TPU v7x, 32 devices: a whole 2x2x4 slice. The times are simulated.
32 devices in a mesh: dp: 8 (over y, x, core), fsdp: 4 (over z).
Axes of the slice: x: 2, y: 2, z: 4, core: 2. Of those that a mesh axis runs over, the one named last changes fastest.
Arguments:
- tokens: bfloat16 [32768, 768], P(('dp', 'fsdp')), may hold values from -6 to 6
- segment: int32 [64, 512], P(('dp', 'fsdp')), may hold values from 0 to 3, never falling along the last dimension, each value on 1 to 256 neighbouring positions
- blocks: float32 [24, 768, 768], P(None, ('dp', 'fsdp')), may hold values from -0.8660254 to 0.8660254
- vectors: float32 [2, 12, 768], P(None, None, ('dp', 'fsdp')), may hold values from -1.2 to 1.2
- owner: int32 [24], replicated, may hold values from 0 to 7, as said below
- left_basis: float32 [40, 8, 96, 768], P('dp', None, 'fsdp'), may hold values from -1 to 1, as said below
- right_basis: float32 [40, 768, 768], P('dp', None, 'fsdp'), may hold values from -1 to 1, as said below
- rot_first: float32 [40, 768, 768], P('dp', None, 'fsdp'), may hold values from -512 to 512
- rot_second: float32 [40, 768, 768], P('dp', None, 'fsdp'), may hold values from 8192 to 32768
- vec_first: float32 [2, 12, 768], P(None, None, ('dp', 'fsdp')), may hold values from -512 to 512
- vec_second: float32 [2, 12, 768], P(None, None, ('dp', 'fsdp')), may hold values from 8192 to 32768
- cotangent: bfloat16 [32768, 768], P(('dp', 'fsdp')), may hold values from -6 to 6
Outputs:
- layer_out: bfloat16 [32768, 768], P(('dp', 'fsdp'))
- input_grad: float32 [32768, 768], P(('dp', 'fsdp'))
- new_blocks: float32 [24, 768, 768], P(None, ('dp', 'fsdp'))
- new_blocks_low: bfloat16 [24, 768, 768], P(None, ('dp', 'fsdp'))
- first_new: float32 [40, 768, 768], P('dp', None, 'fsdp')
- second_new: float32 [40, 768, 768], P('dp', None, 'fsdp')
- vector_first: float32 [2, 12, 768], P(None, None, ('dp', 'fsdp'))
- vector_second: float32 [2, 12, 768], P(None, None, ('dp', 'fsdp'))
- vector_new: float32 [2, 12, 768], P(None, None, ('dp', 'fsdp'))
Inputs may be any that keep to these rules, and one draw needn't show every extreme that they name: `segment`: each row holds 4 segments numbered from 0, never falling along the row, each of 1 to 256 tokens, one of exactly 256. `owner`: no dp index is named by more than 5 blocks, and one is named by exactly 5. `left_basis`: each slot's matrix, read as [768, 768], is orthogonal. `right_basis`: each slot's matrix is orthogonal.
All inputs are finite; a program needn't handle non-finite values.
Results may differ from a plain program's by a relative error of at most 0.02.
Values may be sent and summed in bfloat16 or wider, within the bound.
A program may use at most 320 MiB of HBM per device.

v0:
```python
import functools

import jax
import jax.numpy as jnp
from jax import lax
from jax.experimental import pallas as pl
from jax.experimental.pallas import tpu as pltpu
from jax.sharding import PartitionSpec as P

H = 12
HD = 64
L = 512
STEP = 5
PAIR = 2 * HD
MIB = 1 << 20

beta_one = 0.5
beta_two = 0.5
adam_epsilon = 1e-08
norm_epsilon = 1e-06
matrix_rate = 0.03
vector_rate = 0.2
weight_decay = 0.01
masked_score = -1e30
low = jnp.bfloat16
full = jnp.float32


def dot_nn(a, b):
    return lax.dot_general(a, b, (((1,), (0,)), ((), ())), preferred_element_type=full)


def dot_nt(a, b):
    return lax.dot_general(a, b, (((1,), (1,)), ((), ())), preferred_element_type=full)


def dot_tn(a, b):
    return lax.dot_general(a, b, (((0,), (0,)), ((), ())), preferred_element_type=full)


def gelu_parts(z):
    size = jnp.abs(z) * 0.7071067811865476
    t = 1.0 / (1.0 + 0.3275911 * size)
    bell = jnp.exp(-0.5 * z * z)
    poly = ((((1.061405429 * t - 1.453152027) * t + 1.421413741) * t - 0.284496736) * t + 0.254829592) * t
    half_tail = 0.5 * poly * bell
    phi = jnp.where(z >= 0, 1.0 - half_tail, half_tail)
    return z * phi, phi + z * bell * 0.3989422804014327


def norm_parts(residual):
    average = jnp.mean(residual, axis=-1, keepdims=True)
    centered = residual - average
    inverse = lax.rsqrt(jnp.mean(centered * centered, axis=-1, keepdims=True) + norm_epsilon)
    return centered * inverse, inverse


def norm_back(upstream, unit, inverse, gain):
    scaled = upstream * gain
    return inverse * (
        scaled
        - jnp.mean(scaled, axis=-1, keepdims=True)
        - unit * jnp.mean(scaled * unit, axis=-1, keepdims=True)
    )


def column_sum(values):
    return jnp.sum(values, axis=0, keepdims=True)


def half_masks(dtype):
    lane = lax.broadcasted_iota(jnp.int32, (1, PAIR), 1)
    first = (lane < HD).astype(full)
    return first.astype(dtype), (1.0 - first).astype(dtype)


def segment_bias(seg_column, seg_row):
    return jnp.where(seg_column == seg_row, 0.0, masked_score)


class Place:
    def __init__(self, z_count):
        self.dp, self.z = lax.axis_index("dp"), lax.axis_index("fsdp")
        self.core, self.spot = lax.rem(self.dp, 2), lax.div(self.dp, 2)
        x_step = 1 - 2 * lax.rem(self.spot, 2)
        y_step = 2 - 4 * lax.div(self.spot, 2)
        self.spot_a = self.spot + (1 - self.core) * x_step + self.core * y_step
        self.spot_b = self.spot + self.core * x_step + (1 - self.core) * y_step
        self.spot_ab = self.spot + x_step + y_step
        self.sibling = (self.dp + 1 - 2 * self.core, self.z)
        self.near_a = (2 * self.spot_a + self.core, self.z)
        self.near_b = (2 * self.spot_b + self.core, self.z)
        self.z_count = z_count
        self.zs = [lax.rem(self.z + d, z_count) for d in range(z_count)]
        self.has_up, self.has_down = self.z < z_count - 1, self.z > 0
        self.middle = self.has_up & self.has_down
        self.across = lax.rem(self.z + 2, z_count)
        self.beside = jnp.where(self.z < 2, 1 - self.z, 5 - self.z)

    def line_sends(self, d):
        return {1: self.has_up, 2: self.z >= 0, 3: self.has_down}[d]

    def line_receives(self, d):
        return {1: self.has_down, 2: self.z >= 0, 3: self.has_up}[d]

    def chip_partners(self):
        return [self.sibling, self.near_a, self.near_b]

    def z_partners(self):
        return [(self.dp, other) for other in self.zs[1:]]


def greet(partners):
    barrier = pltpu.get_barrier_semaphore()
    for device in partners:
        pl.semaphore_signal(barrier, inc=1, device_id=device, device_id_type=pl.DeviceIdType.MESH)
    pl.semaphore_wait(barrier, len(partners))


def remote(source, target, send, receive, device):
    return pltpu.make_async_remote_copy(
        src_ref=source,
        dst_ref=target,
        send_sem=send,
        recv_sem=receive,
        device_id=device,
        device_id_type=pl.DeviceIdType.MESH,
    )


def fold(piece):
    half = piece.shape[1] // 2
    return jnp.concatenate([piece[:, :half], piece[:, half:]], axis=0)


def unfold(piece):
    rows = piece.shape[0] // 2
    return jnp.concatenate([piece[:rows], piece[rows:]], axis=1)


def looked_up(ticks, t):
    now = functools.reduce(jnp.logical_or, [t == tick for tick in ticks])
    which = sum(n * (t == tick).astype(jnp.int32) for n, tick in enumerate(ticks))
    return now, which


def run_due(stages, t):
    for ticks, stage in stages:
        if isinstance(t, int):
            if t in ticks:
                stage(ticks.index(t))
            continue
        now, block = looked_up(ticks, t)

        @pl.when(now)
        def _():
            stage(block)


def sum_times(ready):
    opens, cores, seconds = [], [], []
    for tick in ready:
        opens.append(max(tick, opens[-1] + 1) if opens else tick)
        cores.append(max(opens[-1] + 1, cores[-1] + 1) if cores else opens[-1] + 1)
        seconds.append(max(cores[-1] + 3, seconds[-1] + 3) if seconds else cores[-1] + 3)
    thirds = [tick + 2 for tick in seconds]
    return opens, cores, seconds, thirds, [tick + 2 for tick in thirds]


ANNOUNCE, FORWARD, FIRST, SECOND, CLOSE = -4, -2, 2, 4, 6


def sum_scratch(count, part, width, z_count, kind=low):
    piece = (2 * part // z_count, width // 2) if kind == low else (part // z_count, width)
    return [
        pltpu.VMEM((count, 4, part, width), kind),
        pltpu.VMEM((count, 4, part, width), kind),
        pltpu.VMEM((count, 2, part, width), kind),
        pltpu.VMEM((count, part, width), kind),
        pltpu.VMEM((count, z_count) + piece, kind),
        pltpu.VMEM((count, z_count) + piece, kind),
        pltpu.VMEM((count,) + piece, kind),
        pltpu.SemaphoreType.DMA((count,)),
        pltpu.SemaphoreType.DMA((count, 2)),
        pltpu.SemaphoreType.DMA((count, 2, 2)),
        pltpu.SemaphoreType.DMA((count, 2)),
        pltpu.SemaphoreType.DMA((count, 2, z_count)),
        pltpu.SemaphoreType.DMA((count, 2)),
    ]


SUM_REFS = 13


class BlockSum:
    def __init__(self, place, sources, refs, times):
        self.place, self.sources, self.times = place, sources, times
        (self.own, self.c, self.b, self.a, self.zs, self.zr, self.far,
         self.own_sem, self.c_sem, self.b_sem, self.a_sem, self.z_sem, self.far_sem) = refs
        self.count = self.c.shape[0]
        self.kind = self.c.dtype
        self.z_count = self.zs.shape[1]

    def load(self, i, block):
        return pltpu.make_async_copy(block.at[:, self.place.core], self.own.at[i], self.own_sem.at[i])

    def core_copy(self, i, block):
        return remote(
            block.at[:, 1 - self.place.core], self.c.at[i], self.c_sem.at[i, 0], self.c_sem.at[i, 1], self.place.sibling
        )

    def second_copy(self, i, k):
        chunk = self.place.spot_b if k == 0 else self.place.spot_ab
        return remote(
            self.c.at[i, chunk], self.b.at[i, k], self.b_sem.at[i, 0, k], self.b_sem.at[i, 1, k], self.place.near_b
        )

    def third_copy(self, i):
        return remote(
            self.c.at[i, self.place.spot_a], self.a.at[i], self.a_sem.at[i, 0], self.a_sem.at[i, 1], self.place.near_a
        )

    def z_copy(self, i, d):
        other = self.place.zs[d]
        return remote(
            self.zs.at[i, other], self.zr.at[i, self.place.z], self.z_sem.at[i, 0, d],
            self.z_sem.at[i, 1, self.z_count - d], (self.place.dp, other),
        )

    def open(self, i):
        first = 0
        for source in self.sources:
            count = source.shape[0]

            @pl.when((i >= first) & (i < first + count))
            def _():
                block = source.at[jnp.clip(i - first, 0, count - 1)]
                self.core_copy(i, block).start()
                self.load(i, block).start()

            first += count

    def after_core(self, i):
        block = self.sources[0].at[0]
        self.core_copy(i, block).wait()
        self.load(i, block).wait()
        for k in range(4):
            self.c[i, k] = (self.c[i, k].astype(full) + self.own[i, k].astype(full)).astype(self.kind)
        self.second_copy(i, 0).start()
        self.second_copy(i, 1).start()

    def after_second(self, i):
        other, spot = self.place.spot_a, self.place.spot
        self.second_copy(i, 1).wait()
        self.c[i, other] = (self.c[i, other].astype(full) + self.b[i, 1].astype(full)).astype(self.kind)
        self.third_copy(i).start()
        self.second_copy(i, 0).wait()
        self.c[i, spot] = (self.c[i, spot].astype(full) + self.b[i, 0].astype(full)).astype(self.kind)

    def after_third(self, i):
        self.third_copy(i).wait()
        total = self.c[i, self.place.spot].astype(full) + self.a[i].astype(full)
        rows = total.shape[0] // self.z_count
        for k in range(self.z_count):
            piece = total[k * rows : (k + 1) * rows]
            self.zs[i, k] = fold(piece).astype(low) if self.kind == low else piece
        place = self.place
        for d in (1, 3):
            @pl.when(place.line_sends(d))
            def _():
                self.z_copy(i, d).start()

        @pl.when(jnp.logical_not(place.middle))
        def _():
            self.z_copy(i, 2).start()
            self.far_copy(i).start()
            opposite = self.z_count - 1 - place.z
            self.zr[i, opposite] = jnp.zeros(self.zr.shape[2:], self.kind)

    def far_copy(self, i):
        place = self.place
        return remote(
            self.zs.at[i, self.z_count - 1 - place.z], self.far.at[i], self.far_sem.at[i, 0], self.far_sem.at[i, 1],
            (place.dp, place.beside),
        )

    def relay(self, i):
        @pl.when(self.place.middle)
        def _():
            self.far_copy(i).wait_recv()
            across = self.place.across
            self.zs[i, across] = (self.zs[i, across].astype(full) + self.far[i].astype(full)).astype(self.kind)
            self.z_copy(i, 2).start()

    def finish(self, i):
        for d in range(1, self.z_count):
            @pl.when(self.place.line_sends(d))
            def _():
                self.z_copy(i, d).wait_send()

            @pl.when(self.place.line_receives(d))
            def _():
                self.z_copy(i, d).wait_recv()

        @pl.when(jnp.logical_not(self.place.middle))
        def _():
            self.far_copy(i).wait_send()

        total = self.zs[i, self.place.z].astype(full)
        for d in range(1, self.z_count):
            total = total + self.zr[i, self.place.zs[d]].astype(full)
        return total

    def tick(self, t):
        stages = (self.relay, self.after_third, self.after_second, self.after_core, self.open)
        run_due(list(zip(self.times[::-1], stages)), t)

    @property
    def last(self):
        return self.times[4][-1]


class LineGather:
    def __init__(self, place, source, target, first, local_sem, sem, z_count):
        self.place = place
        self.source = source.at[pl.ds(first, target.shape[1])]
        self.target, self.local_sem, self.sem, self.z_count = target, local_sem, sem, z_count

    def hop_copy(self, hop, way):
        dp, z = self.place.dp, self.place.z
        if way == 0:
            piece, other, coming = z - hop + 1, z + 1, z - hop
            sends = (piece >= 0) & (other < self.z_count)
            receives = coming >= 0
        else:
            piece, other, coming = z + hop - 1, z - 1, z + hop
            sends = (piece < self.z_count) & (other >= 0)
            receives = coming < self.z_count
        piece = jnp.clip(piece, 0, self.z_count - 1)
        other = jnp.clip(other, 0, self.z_count - 1)
        source = self.source if hop == 1 else self.target.at[piece]
        copy = remote(source, self.target.at[piece], self.sem.at[way, 0, hop - 1], self.sem.at[way, 1, hop - 1], (dp, other))
        return copy, sends, receives

    def local(self):
        return pltpu.make_async_copy(self.source, self.target.at[self.place.z], self.local_sem)

    def start(self, hop):
        if hop == 1:
            self.local().start()
        for way in range(2):
            copy, sends, _ = self.hop_copy(hop, way)

            @pl.when(sends)
            def _():
                copy.start()

    def wait(self, hop):
        if hop == 1:
            self.local().wait()
        for way in range(2):
            copy, sends, receives = self.hop_copy(hop, way)

            @pl.when(sends)
            def _():
                copy.wait_send()

            @pl.when(receives)
            def _():
                copy.wait_recv()

    def advance(self, hop):
        if hop > 1:
            self.wait(hop - 1)
        if hop < self.z_count:
            self.start(hop)


def gather_scratch(count, rows, width, z_count, kind=low):
    piece = (2 * rows // z_count, width // 2) if kind == low else (rows // z_count, width)
    return [
        pltpu.VMEM((count, z_count) + piece, kind),
        pltpu.SemaphoreType.DMA((count, 2, z_count)),
        pltpu.SemaphoreType.DMA((count, 2)),
        pltpu.SemaphoreType.DMA((count, 2, 2)),
        pltpu.SemaphoreType.DMA((count, 2)),
        pltpu.SemaphoreType.DMA((count, 2)),
    ]


GATHER_REFS = 6


class BlockGather:
    def __init__(self, place, source, whole, base, refs):
        self.place, self.source, self.whole, self.base = place, source, whole, base
        self.zr, self.z_sem, self.a_sem, self.b_sem, self.c_sem, self.far_sem = refs
        self.count, self.z_count = self.zr.shape[0], self.zr.shape[1]

    def z_copy(self, i, d):
        place = self.place
        return remote(
            self.source.at[i], self.zr.at[i, place.z], self.z_sem.at[i, 0, d], self.z_sem.at[i, 1, self.z_count - d],
            (place.dp, place.zs[d]),
        )

    def chunk(self, i, spot):
        return self.whole.at[self.base + i, spot, self.place.core]

    def first_copy(self, i):
        chunk = self.chunk(i, self.place.spot)
        return remote(chunk, chunk, self.a_sem.at[i, 0], self.a_sem.at[i, 1], self.place.near_a)

    def second_copy(self, i, k):
        chunk = self.chunk(i, self.place.spot if k == 0 else self.place.spot_a)
        return remote(chunk, chunk, self.b_sem.at[i, 0, k], self.b_sem.at[i, 1, k], self.place.near_b)

    def core_copy(self, i):
        chunks = self.whole.at[self.base + i, :, self.place.core]
        return remote(chunks, chunks, self.c_sem.at[i, 0], self.c_sem.at[i, 1], self.place.sibling)

    def far_copy(self, i):
        place = self.place
        piece = self.zr.at[i, place.across]
        return remote(piece, piece, self.far_sem.at[i, 0], self.far_sem.at[i, 1], (place.dp, place.beside))

    def announce(self, i):
        for d in range(1, self.z_count):
            @pl.when(self.place.line_sends(d))
            def _():
                self.z_copy(i, d).start()

        self.zr[i, self.place.z] = self.source[i]

    def forward(self, i):
        @pl.when(self.place.middle)
        def _():
            self.z_copy(i, 2).wait_recv()
            self.far_copy(i).start()

    def begin(self):
        for i in range(min(-ANNOUNCE, self.count)):
            self.announce(i)

    def open(self, i):
        place = self.place
        for d in range(1, self.z_count):
            @pl.when(place.line_sends(d))
            def _():
                self.z_copy(i, d).wait_send()

        for d in (1, 3):
            @pl.when(place.line_receives(d))
            def _():
                self.z_copy(i, d).wait_recv()

        @pl.when(place.middle)
        def _():
            self.far_copy(i).wait_send()

        @pl.when(jnp.logical_not(place.middle))
        def _():
            self.z_copy(i, 2).wait_recv()
            self.far_copy(i).wait_recv()

        pieces = [self.zr[i, k].astype(full) for k in range(self.z_count)]
        if self.zr.dtype == low:
            pieces = [unfold(piece) for piece in pieces]
        whole = jnp.concatenate(pieces, axis=0).astype(self.whole.dtype)
        self.whole[self.base + i, self.place.spot, self.place.core] = whole
        self.first_copy(i).start()
        self.second_copy(i, 0).start()

    def after_first(self, i):
        self.first_copy(i).wait()
        self.second_copy(i, 1).start()

    def after_second(self, i):
        self.second_copy(i, 0).wait()
        self.second_copy(i, 1).wait()
        self.core_copy(i).start()

    def close(self, i):
        self.core_copy(i).wait()

    def tick(self, t, done=None):
        def close(i):
            self.close(i)
            if done is not None:
                done(i)

        @pl.when(t == 0)
        def _():
            for i in range(min(-FORWARD, self.count)):
                self.forward(i)

        stages = (
            (SECOND, self.after_second), (FIRST, self.after_first), (0, self.open), (FORWARD, self.forward),
            (ANNOUNCE, self.announce), (CLOSE, close),
        )
        for late, stage in stages:
            @pl.when((t >= max(late, 0)) & (t - late < self.count))
            def _():
                stage(t - late)


def split_refs(refs, *counts):
    result, start = [], 0
    for count in counts:
        result.append(refs[start : start + count])
        start += count
    return result


class Side:
    def __init__(self, plan, sources, targets, sum_refs, line_refs, own=None):
        self.plan = plan
        sums = plan.sums
        blocks = [source.at[pl.ds(plan.skip, source.shape[0] - plan.skip)] for source in sources[:sums]]
        blocks += [own] if plan.own else []
        self.place = Place(plan.z_count) if plan.active else None
        self.sum = BlockSum(self.place, blocks, sum_refs, plan.times) if plan.total else None
        self.result = targets[0] if plan.total else None
        self.lines = line_gathers(self.place, plan.lines, sources[sums:], targets[bool(plan.total) :], line_refs, plan.z_count)

    def enter(self, now):
        if not self.plan.active:
            return

        @pl.when(now)
        def _():
            greet((self.place.chip_partners() if self.plan.total else []) + self.place.z_partners())
            for line in self.lines:
                line.advance(1)

    def tick(self, t):
        if self.plan.total:
            self.sum.tick(t)

    def leave(self, now, ticks):
        if not self.plan.active:
            return

        @pl.when(now)
        def _():
            if self.plan.total:
                if self.sum.last >= ticks:
                    lax.fori_loop(ticks, self.sum.last + 1, lambda t, carry: (self.tick(t), carry)[1], 0)
                for i in range(self.sum.count):
                    self.result[i] = self.sum.finish(i).astype(low)
            for line in self.lines:
                line.advance(self.plan.z_count)

    def advance(self, now, hop):
        if self.lines and hop < self.plan.z_count:
            @pl.when(now)
            def _():
                for line in self.lines:
                    line.advance(hop)


class Plan:
    def __init__(self, pending=None, lines=(), z_count=1, own=0, size=None, ready=(), skip=0):
        self.z_count = z_count
        self.sums = int(pending is not None)
        self.own, self.skip = own, skip
        self.total = own + (pending.shape[0] - skip if self.sums else 0)
        self.times = sum_times(ready) if self.total else None
        self.lines = [(first, count) for _, first, count in lines]
        self.active = bool(self.total or lines)
        self.arguments, self.results, self.result_specs, self.scratch = [], [], [], []
        if self.sums:
            self.arguments.append(pending)
        if self.total:
            part, width = size
            self.results.append(jax.ShapeDtypeStruct((self.total, 2 * part // z_count, width // 2), low))
            self.result_specs.append(
                pl.BlockSpec(self.results[0].shape, lambda i: (0, 0, 0), pipeline_mode=pl.Buffered(1))
            )
            self.scratch += sum_scratch(self.total, part, width, z_count)
        for basis, _, count in lines:
            self.arguments.append(basis)
            self.results.append(jax.ShapeDtypeStruct((z_count, count) + basis.shape[1:], low))
            self.result_specs.append(ANYWHERE)
        self.scratch += line_scratch(len(lines), z_count)
        self.argument_specs = [ANYWHERE] * len(self.arguments)

    def split(self, refs, inputs, outputs, scratch):
        count = len(self.lines)
        return split_refs(
            refs, inputs, self.sums + count, outputs, bool(self.total) + count, scratch,
            SUM_REFS * bool(self.total), 2 * bool(self.lines),
        )


def line_scratch(count, z_count):
    if not count:
        return []
    return [pltpu.SemaphoreType.DMA((count,)), pltpu.SemaphoreType.DMA((count, 2, 2, z_count - 1))]


def line_gathers(place, spans, sources, targets, refs, z_count):
    return [
        LineGather(place, source, target, first, refs[0].at[n], refs[1].at[n], z_count)
        for n, (source, target, (first, _)) in enumerate(zip(sources, targets, spans))
    ]


ANYWHERE = pl.BlockSpec(memory_space=pl.ANY)
IN_VMEM = pl.BlockSpec(memory_space=pltpu.VMEM)


def forward_kernel(plan, *refs):
    inputs, sources, outputs, targets, scratch, gather_refs, vec_refs, line_refs = plan.split(refs)
    x_ref, segc_ref, segr_ref, vec_ref, w_hbm = inputs
    (q_ref, k_ref, v_ref, ctxt_ref, lse_ref, x1_ref, inv1_ref, n1_ref, u_ref, gp_ref, x2_ref, inv2_ref,
     out_ref) = outputs
    w, bias, vt, n1_all, acc, w_sem = scratch
    s = pl.program_id(0)
    tokens, width = acc.shape
    rows_now = x_ref.shape[0]
    rows = tokens // rows_now
    inner = plan.inner
    local = plan.local
    gather = vec_gather = None
    place = Place(plan.z_count) if plan.gathered else None
    if plan.gathered:
        w_out, out_sem = targets[0], scratch_tail(plan, refs)
        gather = BlockGather(place, sources[0], w, local, gather_refs)
        if plan.vectors:
            vec_gather = BlockGather(place, sources[1], plan.vec_whole(refs), 0, vec_refs)
            vec_ref = targets[1]
    lines = line_gathers(place, plan.lines, sources[plan.line_at :], targets[plan.line_target_at :], line_refs, plan.z_count)

    def keep(i):
        return pltpu.make_async_copy(w.at[local + i], w_out.at[i], out_sem.at[i])

    def load(j):
        return pltpu.make_async_copy(w_hbm.at[plan.order[j]], w.at[j], w_sem.at[j])

    def matrix(j):
        return w[j].reshape(width, width)

    def arrive(j):
        if j < local:
            load(j).wait()

    def tick(t):
        if gather is not None:
            gather.tick(t, lambda i: keep(i).start())
            if vec_gather is not None:
                vec_gather.tick(t)

    pairs = width // PAIR
    row_ticks = plan.row_ticks

    @pl.when(s == 0)
    def _():
        for j in range(local):
            load(j).start()
        if gather is not None:
            greet(place.chip_partners() + place.z_partners())
            if vec_gather is not None:
                vec_gather.begin()
            gather.begin()
            lax.fori_loop(0, plan.lead, lambda t, carry: (tick(t), carry)[1], 0)
            for line in lines:
                line.advance(1)
            if vec_gather is not None:
                turned = vec_gather.whole[0].reshape(width, vec_gather.whole.shape[-1]).T
                for layer in range(2):
                    count = plan.vector_rows
                    targets[1 + layer][0:count, :] = turned[layer * count : (layer + 1) * count, :]
        for j in range(min(local, 3)):
            arrive(j)

    @pl.when(s < rows)
    def _():
        xin = x_ref[...].astype(low)
        bias[...] = segment_bias(segc_ref[0], segr_ref[0])
        q_ref[...] = (dot_nn(xin, matrix(0)) + vec_ref[0:1, :]).astype(low)
        k_ref[...] = dot_nn(xin, matrix(1)).astype(low)
        value = dot_nn(xin, matrix(2)) + vec_ref[1:2, :]
        v_ref[...] = value.astype(low)
        vt[...] = value.T.astype(low)
        masks = half_masks(low)

        def pair_step(p, carry):
            lanes = pl.ds(pl.multiple_of(p * PAIR, PAIR), PAIR)
            q_pair = q_ref[:, lanes] * jnp.asarray(HD ** (-0.5), low)
            k_pair = k_ref[:, lanes]
            for h in range(2):
                scores = dot_nt(k_pair, q_pair * masks[h]) + bias[...]
                largest = jnp.max(scores, axis=0, keepdims=True)
                expanded = jnp.exp(scores - largest)
                total = column_sum(expanded)
                here = pl.ds(pl.multiple_of(p * PAIR + h * HD, HD), HD)
                context = dot_nn(vt[here, :], expanded.astype(low)) * (1.0 / total)
                ctxt_ref[here, :] = context.astype(low)
                lse_ref[0, pl.ds(2 * p + h, 1), :] = largest + jnp.log(total)
            if gather is not None:
                spots = [n for n in range(pairs) if (n + 1) * row_ticks // pairs > n * row_ticks // pairs]
                now, which = looked_up(spots, p)

                @pl.when(now)
                def _():
                    tick(plan.lead + s * row_ticks + which)
            return carry

        lax.fori_loop(0, pairs, pair_step, 0)

        @pl.when(s == 0)
        def _():
            if local > 3:
                arrive(3)
            for line in lines:
                line.advance(2)

        context = ctxt_ref[...].astype(full).T.astype(low)
        attended = dot_nn(context, matrix(3)) + vec_ref[2:3, :]
        unit, inverse = norm_parts(x_ref[...].astype(full) + attended)
        x1_ref[...] = unit
        inv1_ref[...] = inverse
        normed = unit * vec_ref[3:4, :] + vec_ref[4:5, :]
        here = pl.ds(pl.multiple_of(s * rows_now, rows_now), rows_now)
        acc[here, :] = normed + vec_ref[5 + inner : 6 + inner, :]
        normed = normed.astype(low)
        n1_ref[...] = normed
        n1_all[here, :] = normed

    tile = tokens // 4
    starts, firsts = plan.step_ticks(rows * row_ticks)

    @pl.when(s >= rows)
    def _():
        c = s - rows

        @pl.when(c == 0)
        def _():
            for j in range(4, local):
                arrive(j)
            for line in lines:
                line.advance(3)

        start = sum(n * (c == k).astype(jnp.int32) for k, n in enumerate(starts))
        first = sum(n * (c == k).astype(jnp.int32) for k, n in enumerate(firsts))
        if gather is not None:
            lax.fori_loop(start, first, lambda t, carry: (tick(t), carry)[1], 0)

        def token_step(i, carry):
            for half in range(2):
                here = pl.ds(pl.multiple_of((2 * i + half) * tile, tile), tile)
                value, slope = gelu_parts(dot_nn(n1_all[here, :], matrix(4 + 2 * c)) + vec_ref[pl.ds(5 + c, 1), :])
                active = value.astype(low)
                u_ref[here, :] = active
                gp_ref[here, :] = slope.astype(low)
                acc[here, :] += dot_nn(active, matrix(5 + 2 * c))
            tick(first + i)
            return carry

        lax.fori_loop(0, 2, token_step, 0)

        @pl.when(c == inner - 1)
        def _():
            base = 5 + inner

            def last(i, carry):
                here = pl.ds(pl.multiple_of(i * tile, tile), tile)
                unit, inverse = norm_parts(acc[here, :])
                x2_ref[here, :] = unit
                inv2_ref[here, :] = inverse
                out_ref[here, :] = (
                    unit * vec_ref[base + 1 : base + 2, :] + vec_ref[base + 2 : base + 3, :]
                ).astype(out_ref.dtype)
                return carry

            lax.fori_loop(0, 4, last, 0)
            if gather is not None:
                last_tick = gather.count - 1 + CLOSE
                lax.fori_loop(firsts[-1] + 2, last_tick + 1, lambda t, carry: (tick(t), carry)[1], 0)
                for line in lines:
                    line.advance(plan.z_count)
                for i in range(gather.count):
                    keep(i).wait()


class ForwardPlan:
    def __init__(self, inner, local, shards=None, vec_shard=None, vector_rows=0, lines=(), lead=0, row_ticks=0, z_count=1):
        self.inner, self.local, self.lead, self.row_ticks, self.z_count = inner, local, lead, row_ticks, z_count
        self.vector_rows = vector_rows
        self.order = [0, 1, 2, 3]
        for c in range(inner):
            self.order += [4 + c, 4 + inner + c]
        self.gathered = 0 if shards is None else shards.shape[0]
        self.vectors = vec_shard is not None
        self.lines = [(first, count) for _, first, count in lines]
        self.line_at = int(self.gathered > 0) + int(self.vectors)
        self.line_target_at = int(self.gathered > 0) + 2 * int(self.vectors)
        self.arguments, self.argument_specs, self.results, self.result_specs, self.scratch = [], [], [], [], []
        shape = jax.ShapeDtypeStruct
        if self.gathered:
            width = 2 * shards.shape[2]
            self.arguments.append(shards)
            self.argument_specs.append(IN_VMEM)
            self.results.append(shape((self.gathered, 4, 2, width // 8, width), low))
            self.result_specs.append(ANYWHERE)
            self.scratch += gather_scratch(self.gathered, width // 8, width, z_count)
        if self.vectors:
            rows, lanes = vec_shard.shape[1:]
            self.arguments.append(vec_shard)
            self.argument_specs.append(IN_VMEM)
            for _ in range(2):
                self.results.append(shape((16, width), full))
                self.result_specs.append(pl.BlockSpec((16, width), lambda s: (0, 0)))
            self.scratch += gather_scratch(1, width // 8, lanes, z_count, full)
        for basis, _, count in lines:
            self.arguments.append(basis)
            self.argument_specs.append(ANYWHERE)
            self.results.append(shape((z_count, count) + basis.shape[1:], low))
            self.result_specs.append(ANYWHERE)
        self.scratch += line_scratch(len(lines), z_count)
        if self.gathered:
            self.scratch.append(pltpu.SemaphoreType.DMA((self.gathered,)))
        if self.vectors:
            self.scratch.append(pltpu.VMEM((1, 4, 2, width // 8, lanes), full))

    def step_ticks(self, row_ticks):
        starts, firsts = [], []
        now = self.lead + row_ticks
        for c in range(self.inner):
            starts.append(now)
            needed = 5 + 2 * c - self.local
            firsts.append(max(now, needed + CLOSE + 1) if self.gathered else now)
            now = firsts[-1] + 2
        return starts, firsts

    def split(self, refs):
        return split_refs(
            refs, 5, len(self.arguments), 13, len(self.results), 6, GATHER_REFS * bool(self.gathered),
            GATHER_REFS * self.vectors, 2 * bool(self.lines),
        )

    def vec_whole(self, refs):
        return refs[-1]


def scratch_tail(plan, refs):
    return refs[-2] if plan.vectors else refs[-1]


def forward_layer(hidden, seg_column, seg_row, vectors, weights, out_dtype, plan, identity=None):
    tokens, width = hidden.shape
    inner = plan.inner
    wide = width * inner
    rows = tokens // L
    heads = width // HD
    shape = jax.ShapeDtypeStruct

    def here(s):
        return jnp.minimum(s, rows - 1)

    def column(s):
        return jnp.maximum(s - rows, 0)

    def row_block(columns):
        return pl.BlockSpec((L, columns), lambda s: (here(s), 0))

    def whole(columns):
        return pl.BlockSpec((tokens, columns), lambda s: (0, 0), pipeline_mode=pl.Buffered(1))

    wide_block = pl.BlockSpec((tokens, width), lambda s: (0, column(s)))
    out_shape = (
        shape((tokens, width), low), shape((tokens, width), low), shape((tokens, width), low),
        shape((width, tokens), low), shape((rows, heads, L), full),
        shape((tokens, width), full), shape((tokens, 1), full), shape((tokens, width), low),
        shape((tokens, wide), low), shape((tokens, wide), low),
        shape((tokens, width), full), shape((tokens, 1), full), shape((tokens, width), out_dtype),
        *plan.results,
    )
    out_specs = (
        row_block(width), row_block(width), row_block(width),
        pl.BlockSpec((width, L), lambda s: (0, here(s))), pl.BlockSpec((1, heads, L), lambda s: (here(s), 0, 0)),
        row_block(width), row_block(1), row_block(width),
        wide_block, wide_block,
        whole(width), whole(1), whole(width),
        *plan.result_specs,
    )
    total = 4 + 2 * inner
    held = max(total, plan.local + plan.gathered)
    return pl.pallas_call(
        functools.partial(forward_kernel, plan),
        grid=(rows + inner,),
        out_shape=out_shape,
        in_specs=[
            row_block(width),
            pl.BlockSpec((1, L, 1), lambda s: (here(s), 0, 0)),
            pl.BlockSpec((1, 1, L), lambda s: (here(s), 0, 0)),
            pl.BlockSpec(vectors.shape, lambda s: (0, 0)),
            ANYWHERE,
            *plan.argument_specs,
        ],
        out_specs=out_specs,
        scratch_shapes=[
            pltpu.VMEM((held, 4, 2, width // 8, width), low),
            pltpu.VMEM((L, L), full),
            pltpu.VMEM((width, L), low),
            pltpu.VMEM((tokens, width), low),
            pltpu.VMEM((tokens, width), full),
            pltpu.SemaphoreType.DMA((total,)),
            *plan.scratch,
        ],
        compiler_params=pltpu.CompilerParams(
            dimension_semantics=("arbitrary",), vmem_limit_bytes=62 * MIB,
            collective_id=identity, has_side_effects=identity is not None,
        ),
        cost_estimate=pl.CostEstimate(
            flops=2 * tokens * width * width * total + 4 * tokens * L * width,
            bytes_accessed=40 * MIB,
            transcendentals=tokens * (L * heads + wide),
        ),
        name="layer_forward",
    )(hidden, seg_column, seg_row, vectors, weights.reshape(-1, 4, 2, width // 8, width), *plan.arguments)


WIDE_HEAD_TICKS, WIDE_STEP_TICKS = 2, 4


def wide_ready(own):
    return [WIDE_HEAD_TICKS + WIDE_STEP_TICKS * (n // 2) + 2 + n % 2 for n in range(own)]


def wide_back_kernel(plan, inner, *refs):
    inputs, sources, outputs, targets, scratch, sum_refs, line_refs = plan.split(refs, 11, 4, 11)
    up_hbm, x2_hbm, inv2_hbm, x1_hbm, inv1_hbm, n1_hbm, vec_ref, wup_ref, wdown_ref, u_ref, gp_ref = inputs
    dw_ref, dr1_ref, da_ref, dvec_ref = outputs
    n1t, dz, kept_dw, up_ref, x2_ref, inv2_ref, x1_ref, inv1_ref, n1_ref, tile_sem, load_sem = scratch
    dy, dn1 = da_ref, dr1_ref
    c = pl.program_id(0)
    steps = pl.num_programs(0)
    tokens, width = dn1.shape
    tile = tokens // 4
    base = 5 + inner
    side = Side(plan, sources, targets, sum_refs, line_refs, kept_dw)

    def tile_copies(i):
        rows = pl.ds(pl.multiple_of(i * tile, tile), tile)
        return [
            pltpu.make_async_copy(source.at[rows], target.at[rows], tile_sem.at[n, i])
            for n, (source, target) in enumerate(((up_hbm, up_ref), (x2_hbm, x2_ref), (inv2_hbm, inv2_ref)))
        ]

    late_copies = [
        pltpu.make_async_copy(source, target, load_sem.at[n])
        for n, (source, target) in enumerate(((n1_hbm, n1_ref), (x1_hbm, x1_ref), (inv1_hbm, inv1_ref)))
    ]

    @pl.when(c == 0)
    def _():
        for i in range(4):
            for copy in tile_copies(i):
                copy.start()
        for copy in late_copies:
            copy.start()

    side.enter(c == 0)

    @pl.when(c == 0)
    def _():
        gain = vec_ref[base + 1 : base + 2, :]

        def body(i, carry):
            for copy in tile_copies(i):
                copy.wait()
            gain_sum, shift_sum, bias_sum = carry
            rows = pl.ds(pl.multiple_of(i * tile, tile), tile)
            upstream = up_ref[rows, :].astype(full)
            unit = x2_ref[rows, :]
            back = norm_back(upstream, unit, inv2_ref[rows, :], gain)
            dn1[rows, :] = back
            branch = back.astype(low)
            dy[rows, :] = branch
            @pl.when(lax.rem(i, 2) == 1)
            def _():
                side.tick(lax.div(i, 2))

            return (
                gain_sum + column_sum(upstream * unit),
                shift_sum + column_sum(upstream),
                bias_sum + column_sum(branch.astype(full)),
            )

        zero = jnp.zeros((1, width), full)
        gain_sum, shift_sum, bias_sum = lax.fori_loop(0, 4, body, (zero, zero, zero))
        dvec_ref[...] = jnp.zeros(dvec_ref.shape, full)
        dvec_ref[base : base + 1, :] = bias_sum
        dvec_ref[base + 1 : base + 2, :] = gain_sum
        dvec_ref[base + 2 : base + 3, :] = shift_sum
        late_copies[0].wait()
        n1t[...] = n1_ref[...].astype(full).T.astype(low)

    first_tick = WIDE_HEAD_TICKS + WIDE_STEP_TICKS * c

    def token_step(i, carry):
        for half in range(2):
            rows = pl.ds(pl.multiple_of((2 * i + half) * tile, tile), tile)
            slope = gp_ref[rows, :].astype(full)
            piece = (dot_nt(dy[rows, :], wdown_ref[0]) * slope).astype(low)
            dz[rows, :] = piece
            dn1[rows, :] += dot_nt(piece, wup_ref[0])
            carry = carry + column_sum(piece.astype(full))
        side.tick(first_tick + i)
        return carry

    bias_sum = lax.fori_loop(0, 2, token_step, jnp.zeros((1, width), full))
    side.advance(c == 1, 2)
    side.advance(c == 3, 3)
    for j in range(inner):
        @pl.when(c == j)
        def _():
            dvec_ref[5 + j : 6 + j, :] = bias_sum

    def store(k, grad):
        if plan.own:
            @pl.when(2 * c + k < plan.own)
            def _():
                kept_dw[2 * c + k] = grad.reshape(kept_dw.shape[1:])

            @pl.when(2 * c + k >= plan.own)
            def _():
                dw_ref[k, 0] = grad
        else:
            dw_ref[k, 0] = grad

    store(0, dot_nn(n1t[...], dz[...]).astype(low))
    side.tick(first_tick + 2)
    store(1, dot_tn(u_ref[...], dy[...]).astype(low))
    side.tick(first_tick + 3)
    final_tick = WIDE_HEAD_TICKS + WIDE_STEP_TICKS * inner

    @pl.when(c == steps - 1)
    def _():
        for copy in late_copies[1:]:
            copy.wait()
        gain = vec_ref[3:4, :]

        def body(i, carry):
            gain_sum, shift_sum, bias_sum = carry
            rows = pl.ds(pl.multiple_of(i * tile, tile), tile)
            upstream = dn1[rows, :]
            unit = x1_ref[rows, :]
            back = norm_back(upstream, unit, inv1_ref[rows, :], gain)
            dr1_ref[rows, :] = back
            branch = back.astype(low)
            da_ref[rows, :] = branch
            @pl.when(lax.rem(i, 2) == 1)
            def _():
                side.tick(final_tick + lax.div(i, 2))

            return (
                gain_sum + column_sum(upstream * unit),
                shift_sum + column_sum(upstream),
                bias_sum + column_sum(branch.astype(full)),
            )

        zero = jnp.zeros((1, width), full)
        gain_sum, shift_sum, bias_sum = lax.fori_loop(0, 4, body, (zero, zero, zero))
        dvec_ref[2:3, :] = bias_sum
        dvec_ref[3:4, :] = gain_sum
        dvec_ref[4:5, :] = shift_sum

    side.leave(c == steps - 1, final_tick + 2)


def wide_back(upstream, kept, vectors, weights, places, plan, identity=None):
    x1, inv1, n1, u, gp, x2, inv2 = kept
    tokens, width = x1.shape
    up_start, down_start, stride = places
    inner = u.shape[1] // width
    shape = jax.ShapeDtypeStruct

    return pl.pallas_call(
        functools.partial(wide_back_kernel, plan, inner),
        grid=(inner,),
        out_shape=(
            shape((2, inner - plan.own // 2, width, width), low),
            shape((tokens, width), full), shape((tokens, width), low), shape((16, width), full),
            *plan.results,
        ),
        in_specs=[
            *[ANYWHERE] * 6,
            pl.BlockSpec(vectors.shape, lambda c: (0, 0), pipeline_mode=pl.Buffered(1)),
            pl.BlockSpec((1, width, width), lambda c: (up_start + stride * c, 0, 0)),
            pl.BlockSpec((1, width, width), lambda c: (down_start + stride * c, 0, 0)),
            pl.BlockSpec((tokens, width), lambda c: (0, c)),
            pl.BlockSpec((tokens, width), lambda c: (0, c)),
            *plan.argument_specs,
        ],
        out_specs=(
            pl.BlockSpec((2, 1, width, width), lambda c: (0, jnp.maximum(c - plan.own // 2, 0), 0, 0)),
            pl.BlockSpec((tokens, width), lambda c: (0, 0), pipeline_mode=pl.Buffered(1)),
            pl.BlockSpec((tokens, width), lambda c: (0, 0), pipeline_mode=pl.Buffered(1)),
            pl.BlockSpec((16, width), lambda c: (0, 0)),
            *plan.result_specs,
        ),
        scratch_shapes=[
            pltpu.VMEM((width, tokens), low),
            pltpu.VMEM((tokens, width), low),
            pltpu.VMEM((plan.own, 4, 2, width // 8, width) if plan.own else (8, 128), low),
            pltpu.VMEM((tokens, width), upstream.dtype),
            pltpu.VMEM((tokens, width), full),
            pltpu.VMEM((tokens, 1), full),
            pltpu.VMEM((tokens, width), full),
            pltpu.VMEM((tokens, 1), full),
            pltpu.VMEM((tokens, width), low),
            pltpu.SemaphoreType.DMA((3, 4)),
            pltpu.SemaphoreType.DMA((3,)),
            *plan.scratch,
        ],
        compiler_params=pltpu.CompilerParams(
            dimension_semantics=("arbitrary",), vmem_limit_bytes=60 * MIB,
            collective_id=identity, has_side_effects=identity is not None,
        ),
        cost_estimate=pl.CostEstimate(
            flops=8 * tokens * width * width * inner, bytes_accessed=50 * MIB, transcendentals=0
        ),
        name="wide_backward",
    )(upstream, x2, inv2, x1, inv1, n1, vectors, weights, weights, u, gp, *plan.arguments)


def attend_back_kernel(plan, *refs):
    inputs, sources, outputs, targets, scratch, sum_refs, line_refs = plan.split(refs, 11, 3, 14)
    da_hbm, dr1_ref, x_ref, q_ref, k_ref, v_ref, ctxt_hbm, lse_ref, segc_ref, segr_ref, w_hbm = inputs
    dw_ref, dx_ref, dvec_ref = outputs
    bias, dctx, kt, delta, dqt, xt, dq_all, dk_all, dv_all, dwo, da_ref, ctxt_ref, w_ref, load_sem = scratch
    r = pl.program_id(0)
    loads = [
        pltpu.make_async_copy(w_hbm.at[plan.start + 3], w_ref.at[3], load_sem.at[0]),
        pltpu.make_async_copy(da_hbm, da_ref, load_sem.at[1]),
        pltpu.make_async_copy(ctxt_hbm, ctxt_ref, load_sem.at[2]),
        pltpu.make_async_copy(w_hbm.at[pl.ds(plan.start, 3)], w_ref.at[pl.ds(0, 3)], load_sem.at[3]),
    ]

    @pl.when(r == 0)
    def _():
        for copy in loads:
            copy.start()

    side = Side(plan, sources, targets, sum_refs, line_refs, dwo)
    side.enter(r == 0)
    tokens, width = dr1_ref.shape
    pairs = width // PAIR
    ticks = pairs + 4

    def tick(n):
        side.tick(r * ticks + n)

    tick(0)
    here = pl.ds(pl.multiple_of(r * tokens, tokens), tokens)

    @pl.when(r == 0)
    def _():
        for copy in loads[:3]:
            copy.wait()
        grad = dot_nn(ctxt_ref[...], da_ref[...]).astype(low)
        if plan.own:
            dwo[0] = grad.reshape(dwo.shape[1:])
        else:
            dw_ref[3] = grad

    xt[:, here] = x_ref[...].astype(low).astype(full).T.astype(low)
    bias[...] = segment_bias(segc_ref[0], segr_ref[0])
    context_grad = dot_nt(da_ref[here, :], w_ref[3]).astype(low)
    dctx[...] = context_grad
    kt[...] = k_ref[...].astype(full).T.astype(low)
    products = context_grad.astype(full) * ctxt_ref[:, here].astype(full).T
    feature = lax.broadcasted_iota(jnp.int32, (16, width), 1)
    head = lax.broadcasted_iota(jnp.int32, (16, width), 0)
    member = ((feature >= head * HD) & (feature < (head + 1) * HD)).astype(full).astype(low)
    high = products.astype(low)
    rest = (products - high.astype(full)).astype(low)
    delta[...] = dot_nt(member, high) + dot_nt(member, rest)
    tick(1)
    masks = half_masks(low)
    scale = HD ** (-0.5)

    def pair_step(p, carry):
        lanes = pl.ds(pl.multiple_of(p * PAIR, PAIR), PAIR)
        q_pair = q_ref[:, lanes] * jnp.asarray(scale, low)
        k_pair = k_ref[:, lanes]
        v_pair = v_ref[:, lanes]
        g_pair = dctx[:, lanes]
        key_grad = jnp.zeros((tokens, PAIR), full)
        value_grad = jnp.zeros((tokens, PAIR), full)
        for h in range(2):
            q_half = q_pair * masks[h]
            g_half = g_pair * masks[h]
            scores = dot_nt(k_pair, q_half) + bias[...]
            attention = jnp.exp(scores - lse_ref[0, pl.ds(2 * p + h, 1), :])
            value_grad = value_grad + dot_nn(attention.astype(low), g_half)
            attention_grad = dot_nt(v_pair, g_half)
            score_grad = (attention * (attention_grad - delta[pl.ds(2 * p + h, 1), :])).astype(low)
            key_grad = key_grad + dot_nn(score_grad, q_half)
            rows = pl.ds(pl.multiple_of(p * PAIR + h * HD, HD), HD)
            dqt[rows, :] = dot_nn(kt[rows, :], score_grad) * scale
        dk_all[here, lanes] = key_grad.astype(low)
        dv_all[here, lanes] = value_grad.astype(low)
        tick(2 + p)
        side.advance((r == 0) & (p == 4), 2)
        side.advance((r == 1) & (p == 3), 3)
        return carry

    lax.fori_loop(0, pairs, pair_step, 0)
    tick(2 + pairs)

    @pl.when(r == 0)
    def _():
        loads[3].wait()

    query_grad = dqt[...].T.astype(low)
    dq_all[here, :] = query_grad
    key_grad = dk_all[here, :]
    value_grad = dv_all[here, :]
    dx_ref[...] = (
        dr1_ref[...]
        + dot_nt(query_grad, w_ref[0])
        + dot_nt(key_grad, w_ref[1])
        + dot_nt(value_grad, w_ref[2])
    )
    tick(3 + pairs)

    @pl.when(r == 0)
    def _():
        dvec_ref[...] = jnp.zeros(dvec_ref.shape, full)

    dvec_ref[0:1, :] += column_sum(query_grad.astype(full))
    dvec_ref[1:2, :] += column_sum(value_grad.astype(full))

    @pl.when(r == pl.num_programs(0) - 1)
    def _():
        for j, grad in enumerate((dq_all, dk_all, dv_all)):
            dw_ref[j] = dot_nn(xt[...], grad[...]).astype(low)
            side.tick(plan.rows * ticks + j)

    side.leave(r == pl.num_programs(0) - 1, plan.rows * ticks + 3)


def attend_back(da, dr1, hidden, kept, seg_column, seg_row, weights, start, plan, identity=None):
    q, k, v, ctxt, lse = kept
    tokens, width = da.shape
    rows = tokens // L
    heads = width // HD
    shape = jax.ShapeDtypeStruct
    plan.start, plan.rows = start, rows

    def row_block():
        return pl.BlockSpec((L, width), lambda r: (r, 0))

    return pl.pallas_call(
        functools.partial(attend_back_kernel, plan),
        grid=(rows,),
        out_shape=(
            shape((4 - plan.own, width, width), low), shape((tokens, width), full), shape((8, width), full),
            *plan.results,
        ),
        in_specs=[
            ANYWHERE,
            row_block(), row_block(), row_block(), row_block(), row_block(),
            ANYWHERE,
            pl.BlockSpec((1, heads, L), lambda r: (r, 0, 0)),
            pl.BlockSpec((1, L, 1), lambda r: (r, 0, 0)),
            pl.BlockSpec((1, 1, L), lambda r: (r, 0, 0)),
            ANYWHERE,
            *plan.argument_specs,
        ],
        out_specs=(
            pl.BlockSpec((4 - plan.own, width, width), lambda r: (0, 0, 0), pipeline_mode=pl.Buffered(1)),
            row_block(),
            pl.BlockSpec((8, width), lambda r: (0, 0)),
            *plan.result_specs,
        ),
        scratch_shapes=[
            pltpu.VMEM((L, L), full),
            pltpu.VMEM((L, width), low),
            pltpu.VMEM((width, L), low),
            pltpu.VMEM((16, L), full),
            pltpu.VMEM((width, L), full),
            pltpu.VMEM((width, tokens), low),
            pltpu.VMEM((tokens, width), low),
            pltpu.VMEM((tokens, width), low),
            pltpu.VMEM((tokens, width), low),
            pltpu.VMEM((1, 4, 2, width // 8, width) if plan.own else (8, 128), low),
            pltpu.VMEM((tokens, width), low),
            pltpu.VMEM((width, tokens), low),
            pltpu.VMEM((4, width, width), low),
            pltpu.SemaphoreType.DMA((4,)),
            *plan.scratch,
        ],
        compiler_params=pltpu.CompilerParams(
            dimension_semantics=("arbitrary",), vmem_limit_bytes=60 * MIB,
            collective_id=identity, has_side_effects=identity is not None,
        ),
        cost_estimate=pl.CostEstimate(
            flops=16 * tokens * width * width + 10 * tokens * L * width,
            bytes_accessed=30 * MIB,
            transcendentals=tokens * L * heads,
        ),
        name="attend_backward",
    )(da, dr1, hidden, q, k, v, ctxt, lse, seg_column, seg_row, weights, *plan.arguments)


def moments(rotated, first, second):
    first_new = beta_one * first + (1.0 - beta_one) * rotated
    second_new = beta_two * second + (1.0 - beta_two) * rotated * rotated
    direction = (
        first_new
        / (1.0 - beta_one**STEP)
        / (jnp.sqrt(second_new / (1.0 - beta_two**STEP)) + adam_epsilon)
    )
    return first_new, second_new, direction


def pack_lanes(piece):
    rows = piece.shape[0] // 2
    return jnp.concatenate([piece[:rows], piece[rows:]], axis=1)


def unpack_lanes(piece):
    columns = piece.shape[1] // 2
    return jnp.concatenate([piece[:, :columns], piece[:, columns:]], axis=0)


def optimizer_kernel(plan, *refs):
    spans = len(plan.spans)
    inputs, ready, dvecs, bases, lines_in, outputs, lines_out, scratch, sum_refs, vec_refs, line_refs = split_refs(
        refs, 6, plan.ready, plan.dvecs, plan.bases, spans, 5, spans, 21, SUM_REFS, SUM_REFS, 2 * bool(spans)
    )
    index_ref, place_ref, tail_hbm, first_hbm, second_hbm, blocks = inputs
    new_ref, low_ref, first_out, second_out, vec_out = outputs
    (store, left, right, first_in, second_in, g_out, g_in, t_out, t_in, e_out, e_in, w_out, w_in, vec_source,
     load_sem, g_sem, t_sem, e_sem, w_sem, left_sem, right_sem) = scratch
    slots, owners = g_in.shape[0], g_in.shape[1]
    z_count = t_in.shape[1]
    place = Place(z_count)
    dp, z = place.dp, place.z
    dps = [lax.rem(dp + d, owners) for d in range(owners)]
    count = blocks.shape[0]
    many = tail_hbm.shape[0]
    tail_times = [[many * stage + n for n in range(many)] for stage in range(5)]
    tail = BlockSum(place, [tail_hbm], sum_refs, tail_times)
    vec = BlockSum(place, [vec_source], vec_refs, [[many * stage + 1] for stage in range(5)])
    order = plan.free + [s for s in range(slots) if s not in plan.free]
    lines = line_gathers(place, plan.spans, lines_in, lines_out, line_refs, z_count)
    every = list(bases) + list(lines_out)
    late = [s for s in range(slots) if plan.left_map[s][0] >= len(bases)]

    def load(refs_map, target, sem, s):
        n, at = refs_map[s]
        return pltpu.make_async_copy(every[n].at[:, at], target.at[:, s], sem.at[s])

    def load_first(s):
        return pltpu.make_async_copy(first_hbm.at[s], first_in.at[s], load_sem.at[0, s])

    def load_second(s):
        return pltpu.make_async_copy(second_hbm.at[s], second_in.at[s], load_sem.at[1, s])

    for s in order:
        load(plan.right_map, right, right_sem, s).start()
        if s not in late:
            load(plan.left_map, left, left_sem, s).start()
        load_first(s).start()
        load_second(s).start()
    greet([(other, z) for other in dps[1:]] + place.z_partners())
    start = many
    for part in ready:
        store[start : start + part.shape[0]] = part[...]
        start += part.shape[0]
    store[0:many] = jnp.zeros((many,) + store.shape[1:], low)
    store[count] = jnp.zeros(store.shape[1:], low)
    rows = plan.vector_rows
    stacked = jnp.concatenate(
        [dvecs[0][0:2, :], dvecs[1][2:rows, :], dvecs[2][0:2, :], dvecs[3][2:rows, :],
         jnp.zeros((vec_source.shape[-1] - 2 * rows, blocks.shape[2]), full)], axis=0
    )
    vec_source[0] = stacked.T.reshape(vec_source.shape[1:])

    def g_copy(s, d):
        other = dps[d]
        return remote(g_out.at[s, d], g_in.at[s, dp], g_sem.at[0, s, d], g_sem.at[1, s, owners - d], (other, z))

    def t_copy(s, d):
        other = place.zs[d]
        return remote(t_out.at[s, d], t_in.at[s, z], t_sem.at[0, s, d], t_sem.at[1, s, z_count - d], (dp, other))

    def e_copy(s, d):
        other = place.zs[d]
        return remote(e_out.at[s, d], e_in.at[s, z], e_sem.at[0, s, d], e_sem.at[1, s, z_count - d], (dp, other))

    def w_copy(s, d):
        other = dps[d]
        return remote(
            w_out.at[s, other], w_in.at[s * owners + dp], w_sem.at[0, s, d], w_sem.at[1, s, owners - d], (other, z)
        )

    def send_out(s):
        for d in range(1, owners):
            g_out[s, d] = store[index_ref[s * owners + dps[d]]]
            g_copy(s, d).start()
        g_in[s, dp] = store[index_ref[s * owners + dp]]

    def turn(s):
        for d in range(1, owners):
            g_copy(s, d).wait()
        load(plan.right_map, right, right_sem, s).wait()
        grad = jnp.concatenate([unfold(g_in[s, c].astype(full)) for c in range(owners)], axis=0).astype(low)
        for d in range(1, z_count):
            t_out[s, d] = pack_lanes(dot_nt(right[place.zs[d], s], grad)).astype(low)
            t_copy(s, d).start()
        t_in[s, z] = pack_lanes(dot_nt(right[z, s], grad)).astype(low)

    def adapt(s):
        for d in range(1, z_count):
            t_copy(s, d).wait()
        load_first(s).wait()
        load_second(s).wait()
        load(plan.left_map, left, left_sem, s).wait()
        rotated = jnp.zeros(first_in.shape[1:], full)
        for f in range(z_count):
            rotated = rotated + dot_nn(unpack_lanes(t_in[s, f].astype(full)).astype(low), left[f, s])
        first_new, second_new, direction = moments(rotated, first_in[s], second_in[s])
        first_out[s] = first_new
        second_out[s] = second_new
        direction = direction.astype(low)
        for d in range(1, z_count):
            e_out[s, d] = pack_lanes(dot_nt(left[place.zs[d], s], direction)).astype(low)
            e_copy(s, d).start()
        e_in[s, z] = pack_lanes(dot_nt(left[z, s], direction)).astype(low)

    def step_back(s):
        for d in range(1, z_count):
            e_copy(s, d).wait()
        step = jnp.zeros((left.shape[2], left.shape[3]), full)
        for f in range(z_count):
            step = step + dot_nn(unpack_lanes(e_in[s, f].astype(full)).astype(low), right[f, s])
        share = step.shape[0] // owners
        for c in range(owners):
            w_out[s, c] = fold(step[c * share : (c + 1) * share]).astype(low)
        for d in range(1, owners):
            w_copy(s, d).start()
        w_in[s * owners + dp] = w_out[s, dp]

    def sums(stage):
        for t in range(many * stage, many * (stage + 1)):
            tail.tick(t)
            vec.tick(t)

    free = plan.free
    def advance(hop):
        for line in lines:
            line.advance(hop)

    sums(0)
    advance(1)
    for s in free:
        send_out(s)
    sums(1)
    for s in free:
        turn(s)
    sums(2)
    advance(2)
    for s in free:
        adapt(s)
    sums(3)
    sums(4)
    advance(3)
    for i in range(many):
        store[i] = tail.finish(i).astype(low)
    rest = order[len(free) :]
    for s in rest[:2]:
        send_out(s)
    for s in free:
        step_back(s)
    advance(z_count)
    for s in late:
        load(plan.left_map, left, left_sem, s).start()
    for k in range(len(rest) + 2):
        if k < len(rest):
            turn(rest[k])
            if k + 2 < len(rest):
                send_out(rest[k + 2])
        if 0 <= k - 1 < len(rest):
            adapt(rest[k - 1])
        if 0 <= k - 2 < len(rest):
            step_back(rest[k - 2])

    vec_out[...] = vec.finish(0)
    for s in range(slots):
        for d in range(1, owners):
            w_copy(s, d).wait()

    def block_step(b, carry):
        step = unfold(w_in[place_ref[b]].astype(full))
        block = blocks[b]
        new = block - matrix_rate * (step + weight_decay * block)
        new_ref[b] = new
        low_ref[b] = new.astype(low)
        return carry

    lax.fori_loop(0, count, block_step, 0)


class OptimizerPlan:
    def __init__(self, ready, dvecs, bases, spans, left_map, right_map, free, vector_rows):
        self.ready, self.dvecs, self.bases, self.spans = ready, dvecs, bases, spans
        self.left_map, self.right_map, self.free, self.vector_rows = left_map, right_map, free, vector_rows


def optimizer(
    index, places, tail, ready, dvecs, vector_rows, bases, lines, left_map, right_map, free, first, second, blocks,
    z_count, identity,
):
    slots, columns, width = first.shape
    owners = index.shape[0] // slots
    count, rows = blocks.shape[0], blocks.shape[1]
    span = bases[0].shape[2]
    lanes = 128
    shape = jax.ShapeDtypeStruct
    piece = (2 * rows, width // 2)
    tile = (span // 2, 2 * columns)
    smem = pl.BlockSpec(memory_space=pltpu.SMEM)
    spans = [(first_slot, amount) for _, first_slot, amount in lines]
    plan = OptimizerPlan(len(ready), len(dvecs), len(bases), spans, left_map, right_map, free, vector_rows)
    line_shapes = [shape((z_count, amount) + basis.shape[1:], low) for basis, _, amount in lines]
    return pl.pallas_call(
        functools.partial(optimizer_kernel, plan),
        out_shape=(
            shape(blocks.shape, full), shape(blocks.shape, low), shape(first.shape, full), shape(first.shape, full),
            shape((rows, lanes), full), *line_shapes,
        ),
        in_specs=[smem, smem, ANYWHERE, ANYWHERE, ANYWHERE, IN_VMEM]
        + [IN_VMEM] * (len(ready) + len(dvecs)) + [ANYWHERE] * (len(bases) + len(lines)),
        out_specs=(IN_VMEM,) * 5 + (ANYWHERE,) * len(lines),
        scratch_shapes=[
            pltpu.VMEM((count + 1,) + piece, low),
            pltpu.VMEM((z_count, slots, span, width), low),
            pltpu.VMEM((z_count, slots, columns, width), low),
            pltpu.VMEM((slots, columns, width), full),
            pltpu.VMEM((slots, columns, width), full),
            pltpu.VMEM((slots, owners) + piece, low),
            pltpu.VMEM((slots, owners) + piece, low),
            pltpu.VMEM((slots, z_count) + tile, low),
            pltpu.VMEM((slots, z_count) + tile, low),
            pltpu.VMEM((slots, z_count) + tile, low),
            pltpu.VMEM((slots, z_count) + tile, low),
            pltpu.VMEM((slots, owners) + piece, low),
            pltpu.VMEM((slots * owners,) + piece, low),
            pltpu.VMEM((1, owners // 2, 2, width // owners, lanes), full),
            pltpu.SemaphoreType.DMA((2, slots)),
            pltpu.SemaphoreType.DMA((2, slots, owners)),
            pltpu.SemaphoreType.DMA((2, slots, z_count)),
            pltpu.SemaphoreType.DMA((2, slots, z_count)),
            pltpu.SemaphoreType.DMA((2, slots, owners)),
            pltpu.SemaphoreType.DMA((slots,)),
            pltpu.SemaphoreType.DMA((slots,)),
            *sum_scratch(tail.shape[0], tail.shape[3], width, z_count),
            *sum_scratch(1, width // owners, lanes, z_count, full),
            *line_scratch(len(lines), z_count),
        ],
        compiler_params=pltpu.CompilerParams(
            vmem_limit_bytes=60 * MIB, collective_id=identity, has_side_effects=True
        ),
        cost_estimate=pl.CostEstimate(
            flops=8 * slots * span * width * width, bytes_accessed=40 * MIB, transcendentals=slots * width * columns
        ),
        name="optimizer",
    )(index, places, tail, first, second, blocks, *ready, *dvecs, *bases, *[basis for basis, _, _ in lines])


def slot_table(owner, slots, owner_rows):
    block_count = owner.shape[0]
    same_owner = owner[:, None] == owner[None, :]
    ordering = jnp.arange(block_count, dtype=jnp.int32)
    earlier = ordering[None, :] < ordering[:, None]
    ranking = jnp.sum(jnp.where(same_owner & earlier, 1, 0), axis=1).astype(jnp.int32)
    owner_match = owner[None, :] == jnp.arange(owner_rows, dtype=jnp.int32)[:, None]
    slot_match = ranking[None, :] == jnp.arange(slots, dtype=jnp.int32)[:, None]
    return jnp.where(slot_match[:, None, :] & owner_match[None, :, :], 1.0, 0.0).astype(full)


def scatter_sum(grads):
    blocks, width = grads.shape[0], grads.shape[2]
    cut = grads.reshape(blocks, lax.axis_size("dp"), -1, width).transpose(1, 0, 2, 3)
    outer = lax.psum_scatter(cut, "dp", scatter_dimension=0, tiled=False)
    blocks, rows, width = outer.shape
    count = lax.axis_size("fsdp")
    cut = outer.reshape(blocks, count, rows // count, width).transpose(1, 0, 2, 3)
    return lax.psum_scatter(cut, "fsdp", scatter_dimension=0, tiled=False)


def scatter_vectors(grads):
    rows, width = grads.shape
    count = lax.axis_size("dp") * lax.axis_size("fsdp")
    cut = grads.reshape(rows, count, width // count).transpose(1, 0, 2)
    return lax.psum_scatter(cut, ("dp", "fsdp"), scatter_dimension=0, tiled=False)


def gathering_program(
    tokens, segment, blocks, vectors, owner, left_basis, right_basis, rot_first, rot_second, cotangent, z_count
):
    layers, vector_rows = vectors.shape[:2]
    count, shard_rows, width = blocks.shape
    per_layer = count // layers
    inner = (per_layer - 4) // 2
    owners = lax.axis_size("dp")
    slots = rot_first.shape[0]
    part = width // owners
    lanes = 128
    seg_column, seg_row = segment[:, :, None], segment[:, None, :]

    order = [0, 1, 2, 3]
    for c in range(inner):
        order += [4 + c, 4 + inner + c]
    folded = blocks.astype(low).reshape(count, shard_rows, 2, width // 2).transpose(0, 2, 1, 3)
    folded = folded.reshape(count, 2 * shard_rows, width // 2)

    def pick(numbers):
        return jnp.stack([folded[j] for j in numbers])

    head = pick(order + [per_layer + j for j in order[:4]])
    rest = pick([per_layer + j for j in order[4:]])
    vec_shard = vectors.astype(low).astype(full).reshape(layers * vector_rows, shard_rows).T
    vec_shard = jnp.pad(vec_shard, ((0, 0), (0, lanes - layers * vector_rows)))[None]
    left_low = left_basis.reshape(slots, -1, width).astype(low)
    right_low = right_basis.transpose(0, 2, 1).astype(low)

    plan = ForwardPlan(
        inner, 0, head, vec_shard, vector_rows, [(right_low, 0, 2)], lead=9, row_ticks=3, z_count=z_count
    )
    empty_vec = jnp.zeros((16, width), full)
    results = forward_layer(tokens, seg_column, seg_row, empty_vec, jnp.zeros((1, width, width), low), full, plan, 6)
    kept_a = results[:12]
    hidden, weights_a, vec_a, vec_b, right_01 = results[12:]
    weights_a = weights_a.reshape(-1, width, width)
    plan = ForwardPlan(inner, 4, rest, lines=[(right_low, 2, 2)], lead=0, row_ticks=4, z_count=z_count)
    plan.order = [per_layer + j for j in range(4)]
    results = forward_layer(hidden, seg_column, seg_row, vec_b, weights_a, low, plan, 7)
    kept_b = results[:12]
    layer_out, weights_b, right_23 = results[12:]
    weights_b = weights_b.reshape(-1, width, width)

    def cut(grads):
        return grads.reshape(-1, owners // 2, 2, part, width)

    size = (part, width)
    own = 3
    skip = own % 2
    pending = 2 * inner - own

    plan = Plan(None, [(right_low, 4, 1), (left_low, 3, 1)], z_count, own, size, wide_ready(own))
    dw_wide, dr1, da, dvec_wide_b, wide_sum_b, right_4, left_3 = wide_back(
        cotangent, kept_b[5:], vec_b, weights_b, (0, 1, 2), plan, 1
    )
    ready = list(range(pending + 1))
    plan = Plan(cut(dw_wide), [(left_low, 4, 1)], z_count, 1, size, ready, skip)
    dw_attend, upstream, dvec_attend_b, attend_sum_b, left_4 = attend_back(
        da, dr1, hidden, kept_b[:5], seg_column, seg_row, weights_a, per_layer, plan, 2
    )
    plan = Plan(cut(dw_attend), [(left_low, 0, 1)], z_count, own, size, [0, 1, 2] + wide_ready(own))
    dw_wide, dr1, da, dvec_wide_a, wide_sum_a, left_0 = wide_back(
        upstream, kept_a[5:], vec_a, weights_a, (4, 5, 2), plan, 3
    )
    plan = Plan(cut(dw_wide), [(left_low, 1, 1)], z_count, 1, size, ready, skip)
    dw_attend, upstream, dvec_attend_a, attend_sum_a, left_1 = attend_back(
        da, dr1, tokens, kept_a[:5], seg_column, seg_row, weights_a, 0, plan, 5
    )

    three = list(range(3))
    early = [4 + n // 2 + inner * (n % 2) for n in range(own)]
    late = [4 + c + inner * k for k in range(2) for c in range(inner) if 2 * c + k >= own] + [3]
    held_order = three + late + [per_layer + j for j in three] + early + [per_layer + j for j in late + early]
    rank = jnp.asarray([held_order.index(j) for j in range(count)], jnp.int32)
    table = slot_table(owner, slots, owners).reshape(slots * owners, count)
    held = jnp.sum(table, axis=1)
    index = jnp.where(held > 0, jnp.sum(table * rank, axis=1), count).astype(jnp.int32)
    places = jnp.sum(table * jnp.arange(slots * owners, dtype=jnp.int32)[:, None], axis=0).astype(jnp.int32)
    bases = (right_01, right_23, right_4, left_0, left_1, left_3, left_4)
    right_map = [(0, 0), (0, 1), (1, 0), (1, 1), (2, 0)]
    left_map = [(3, 0), (4, 0), (7, 0), (5, 0), (6, 0)]
    free = list(range(3, slots))
    new_blocks, new_low, first_new, second_new, vec_sum, _ = optimizer(
        index, places, cut(dw_attend), (attend_sum_a, wide_sum_a, attend_sum_b, wide_sum_b),
        (dvec_attend_a, dvec_wide_a, dvec_attend_b, dvec_wide_b), vector_rows, bases, [(left_low, 2, 1)], left_map, right_map, free,
        rot_first.transpose(0, 2, 1), rot_second.transpose(0, 2, 1), blocks, z_count, 4,
    )
    first_new, second_new = first_new.transpose(0, 2, 1), second_new.transpose(0, 2, 1)
    vector_grad = vec_sum[:, : layers * vector_rows].T.reshape(layers, vector_rows, shard_rows)
    return layer_out, upstream, new_blocks, new_low, first_new, second_new, vector_grad


def plain_program(
    tokens, segment, blocks, vectors, owner, left_basis, right_basis, rot_first, rot_second, cotangent
):
    layers, vector_rows = vectors.shape[:2]
    per_layer = blocks.shape[0] // layers
    inner = (per_layer - 4) // 2
    width = blocks.shape[2]
    owner_rows = lax.axis_size("dp")
    slots = rot_first.shape[0]
    selector = slot_table(owner, slots, owner_rows)
    vector_parts = lax.all_gather(vectors.astype(low), ("dp", "fsdp"), axis=0, tiled=False)
    vector_full = vector_parts.transpose(1, 2, 0, 3).reshape(layers, vector_rows, width).astype(full)
    blocks_low, vector_full = lax.optimization_barrier((blocks.astype(low), vector_full))

    seg_column = segment[:, :, None]
    seg_row = segment[:, None, :]
    state = tokens
    kept = []
    for layer_index in range(layers):
        start = per_layer * layer_index
        weights = lax.all_gather(blocks_low[start : start + per_layer], ("dp", "fsdp"), axis=1, tiled=True)
        out_dtype = low if layer_index == layers - 1 else full
        results = forward_layer(
            state, seg_column, seg_row, vector_full[layer_index], weights, out_dtype, ForwardPlan(inner, per_layer)
        )
        kept.append((state, weights, results[:5], results[5:12]))
        state = results[12]
    layer_out = state
    upstream = cotangent
    right_low = lax.all_gather(right_basis.astype(low), "fsdp", axis=2, tiled=True)
    block_shards = [None] * layers
    vector_shards = [None] * layers
    for layer_index in reversed(range(layers)):
        hidden, weights, attend_kept, wide_kept = kept[layer_index]
        dw_wide, dr1, da, dvec_wide = wide_back(
            upstream, wide_kept, vector_full[layer_index], weights, (4, 4 + inner, 1), Plan()
        )
        wide_shard = scatter_sum(dw_wide.reshape(-1, width, width))
        dw_attend, upstream, dvec_attend = attend_back(
            da, dr1, hidden, attend_kept, seg_column, seg_row, weights, 0, Plan()
        )
        dvec = jnp.concatenate([dvec_attend[:2], dvec_wide[2:vector_rows]], axis=0)
        block_shards[layer_index] = jnp.concatenate([scatter_sum(dw_attend), wide_shard], axis=0)
        vector_shards[layer_index] = scatter_vectors(dvec)
    vector_grad = jnp.stack(vector_shards)
    block_grad = jnp.concatenate(block_shards, axis=0)
    outgoing = jnp.einsum("srk,kid->srid", selector.astype(low), block_grad, preferred_element_type=full)
    incoming = lax.all_to_all(outgoing.astype(low), "dp", split_axis=1, concat_axis=1, tiled=True)
    owned = incoming.reshape(slots, -1, width)
    turned = jnp.einsum("sik,skj->sij", owned, right_low, preferred_element_type=full).astype(low)
    left_rows = left_basis.reshape(slots, -1, width).astype(low)
    partial_sums = jnp.einsum("sra,srb->sab", left_rows, turned, preferred_element_type=full)
    rotated = lax.psum_scatter(
        partial_sums.astype(low), "fsdp", scatter_dimension=2, tiled=True
    ).astype(full)
    first_new, second_new, direction = moments(rotated, rot_first, rot_second)
    direction_full = lax.all_gather(direction.astype(low), "fsdp", axis=2, tiled=True)
    back_right = jnp.einsum("sab,scb->sac", direction_full, right_low, preferred_element_type=full)
    step_rows = jnp.einsum(
        "sia,sac->sic", left_rows, back_right.astype(low), preferred_element_type=full
    )
    returned = lax.all_to_all(
        step_rows.reshape(slots, owner_rows, -1, width).astype(low),
        "dp",
        split_axis=1,
        concat_axis=1,
        tiled=True,
    )
    step_shard = jnp.einsum("srk,srid->kid", selector.astype(low), returned, preferred_element_type=full)
    new_blocks = blocks - matrix_rate * (step_shard + weight_decay * blocks)
    return layer_out, upstream, new_blocks, new_blocks.astype(low), first_new, second_new, vector_grad


def shards(
    tokens,
    segment,
    blocks,
    vectors,
    owner,
    left_basis,
    right_basis,
    rot_first,
    rot_second,
    vec_first,
    vec_second,
    cotangent,
):
    operands = (
        tokens, segment, blocks, vectors, owner, left_basis, right_basis, rot_first, rot_second, cotangent
    )
    z_count = lax.axis_size("fsdp")
    if lax.axis_size("dp") == 8 and z_count == 4:
        results = gathering_program(*operands, z_count)
    else:
        results = plain_program(*operands)
    layer_out, upstream, new_blocks, new_low, first_new, second_new, vector_grad = results
    vector_first = beta_one * vec_first + (1.0 - beta_one) * vector_grad
    vector_second = beta_two * vec_second + (1.0 - beta_two) * vector_grad * vector_grad
    vector_step = (
        vector_first
        / (1.0 - beta_one**STEP)
        / (jnp.sqrt(vector_second / (1.0 - beta_two**STEP)) + adam_epsilon)
    )
    vector_new = vectors - vector_rate * (vector_step + weight_decay * vectors)
    return (
        layer_out,
        upstream,
        new_blocks,
        new_low,
        first_new,
        second_new,
        vector_first,
        vector_second,
        vector_new,
    )


def solution(mesh):
    return jax.shard_map(
        shards,
        mesh=mesh,
        in_specs=(
            P(("dp", "fsdp"), None),
            P(("dp", "fsdp"), None),
            P(None, ("dp", "fsdp"), None),
            P(None, None, ("dp", "fsdp")),
            P(),
            P("dp", None, "fsdp", None),
            P("dp", None, "fsdp"),
            P("dp", None, "fsdp"),
            P("dp", None, "fsdp"),
            P(None, None, ("dp", "fsdp")),
            P(None, None, ("dp", "fsdp")),
            P(("dp", "fsdp"), None),
        ),
        out_specs=(
            P(("dp", "fsdp"), None),
            P(("dp", "fsdp"), None),
            P(None, ("dp", "fsdp"), None),
            P(None, ("dp", "fsdp"), None),
            P("dp", None, "fsdp"),
            P("dp", None, "fsdp"),
            P(None, None, ("dp", "fsdp")),
            P(None, None, ("dp", "fsdp")),
            P(None, None, ("dp", "fsdp")),
        ),
        check_vma=False,
    )
```

profile of v0, /device:TPU:0, one launch (start us, length us, event | category | flops | bytes accessed | tf_op | source)
XLA Modules:
  0.0 590.8 jit_solution(11695664985870893752)
XLA Ops:
  0.6 1.6 convert_element_type.40
  2.2 0.0 copy-start.7
  2.2 0.0 copy-start.1
  2.2 0.1 copy.76
  2.4 0.1 fusion.7
  2.7 0.0 copy-start.11
  2.7 0.8 copy-done.11
  3.5 0.0 copy-done.7
  3.5 0.0 copy-start.6
  3.5 1.0 copy.44.refs_1_.refs_8_
  4.6 0.6 broadcast_in_dim.47.refs_2_.refs_9_
  5.2 0.0 copy-done.1
  5.2 1.3 convert_bitcast_fusion.refs_7_.refs_6_.refs_11_
  6.4 0.0 copy-done.6
  6.4 0.1 copy.56
  6.5 0.1 reshape.151
  6.6 0.6 bitcast_convert_fusion.refs_6_
  7.2 1.1 reshape.140.refs_4_
  8.3 0.6 broadcast_in_dim.48.refs_3_
  9.0 116.2 %layer_forward.2 = (bf16[1024,768]{1,0:T(8,128)(2,1)}, bf16[1024,768]{1,0:T(8,128)(2,1)}, bf16[1024,768]{1,0:T(8,128)(2,1)}, bf16[768,1024]{1,0:T(8,128)(2,1)}, ...) custom-call(bf16[1024,768]{1,0:T(8,128)(2,1)} %refs_2_.1, ...), custom_call_target="tpu_custom_call" | custom-call | flops 16106127360 | bytes 41943040 | tf_op jit(solution)/shard_map/layer_forward/pallas_call | solution.py:890
  125.3 0.0 copy-start.10
  125.3 0.7 copy-done.10
  126.0 83.5 %layer_forward.3 = (bf16[1024,768]{1,0:T(8,128)(2,1)}, bf16[1024,768]{1,0:T(8,128)(2,1)}, bf16[1024,768]{1,0:T(8,128)(2,1)}, bf16[768,1024]{1,0:T(8,128)(2,1)}, ...) custom-call(f32[1024,768]{1,0:T(8,128)} %get-tuple-element.69.refs_0, ...), custom_call_target="tpu_custom_call" | custom-call | flops 16106127360 | bytes 41943040 | tf_op jit(solution)/shard_map/layer_forward/pallas_call | solution.py:890
  209.6 3.1 convert_element_type.44
  212.7 60.2 %wide_backward.2 = (bf16[2,3,768,768]{3,2,1,0:T(8,128)(2,1)}, f32[1024,768]{1,0:T(8,128)}, bf16[1024,768]{1,0:T(8,128)(2,1)}, f32[16,768]{1,0:T(8,128)}, bf16[3,...) custom-call(bf16[1024,768]{1,0:T(8,128)(2,1)} %refs_0_.3, ...), custom_call_target="tpu_custom_call" | custom-call | flops 19327352832 | bytes 52428800 | tf_op jit(solution)/shard_map/wide_backward/pallas_call | solution.py:1081
  272.9 63.5 %attend_backward.2 = (bf16[3,768,768]{2,1,0:T(8,128)(2,1)}, f32[1024,768]{1,0:T(8,128)}, f32[8,768]{1,0:T(8,128)}, bf16[6,48,384]{2,1,0:T(8,128)(2,1)}, bf16[4,1,192,768]{3,2,1,0:T(8,128)(2,1)}) custom-call(bf16[1024,768]{1,0:T(8,128)(2,1)} %get-tuple-element.81.refs_0_, f32[1024,768]{1,0:T(8,128)} %get-tuple-element.82.refs_1_, ...), custom_call_target="tpu_custom_call" | custom-call | flops 13690208256 | bytes 31457280 | tf_op jit(solution)/shard_map/attend_backward/pallas_call | solution.py:1258
  336.4 63.8 %wide_backward.3 = (bf16[2,3,768,768]{3,2,1,0:T(8,128)(2,1)}, f32[1024,768]{1,0:T(8,128)}, bf16[1024,768]{1,0:T(8,128)(2,1)}, f32[16,768]{1,0:T(8,128)}, bf16[6,...) custom-call(f32[1024,768]{1,0:T(8,128)} %get-tuple-element.89.refs_0_, f32[1024,768]{1,0:T(8,128)} %get-tuple-element.90.refs_1_, ...), custom_call_target="tpu_custom_call" | custom-call | flops 19327352832 | bytes 52428800 | tf_op jit(solution)/shard_map/wide_backward/pallas_call | solution.py:1081
  400.2 0.0 copy-start.13
  400.3 0.0 copy-start.12
  400.3 63.1 %attend_backward.3 = (bf16[3,768,768]{2,1,0:T(8,128)(2,1)}, f32[1024,768]{1,0:T(8,128)}, f32[8,768]{1,0:T(8,128)}, bf16[6,48,384]{2,1,0:T(8,128)(2,1)}, bf16[4,1,192,768]{3,2,1,0:T(8,128)(2,1)}) custom-call(bf16[1024,768]{1,0:T(8,128)(2,1)} %get-tuple-element.99.refs_0_, f32[1024,768]{1,0:T(8,128)} %get-tuple-element.100.refs_1_, bf16[1024,768]{1,0:T(8,128)(2,1)} %refs_2_.1, ...), custom_call_target="tpu_custom_call" | custom-call | flops 13690208256 | bytes 31457280 | tf_op jit(solution)/shard_map/attend_backward/pallas_call | solution.py:1258
  463.4 0.0 copy-done.13
  463.4 0.2 select_reduce_fusion.1
  463.6 0.0 copy-done.12
  463.7 0.1 fusion.1
  463.8 0.6 convert_element_type.48.refs_0_
  464.4 0.5 convert_element_type.50.refs_1_
  464.9 0.0 copy-start.8
  464.9 0.0 copy-start.9
  464.9 110.2 %optimizer.1 = (f32[24,24,768]{2,1,0:T(8,128)}, bf16[24,24,768]{2,1,0:T(8,128)(2,1)}, f32[5,192,768]{2,1,0:T(8,128)}, f32[5,192,768]{2,1,0:T(8,128)}, f32[24,128...) custom-call(s32[40]{0:T(128)} %convert_element_type.48.refs_0_, s32[24]{0:T(128)} %convert_element_type.50.refs_1_, ...), custom_call_target="tpu_custom_call" | custom-call | flops 4529848320 | bytes 41943040 | tf_op jit(solution)/shard_map/optimizer/pallas_call | solution.py:1533
  575.1 0.0 copy-start
  575.2 0.9 slice_bitcast_fusion
  576.0 0.1 copy.49
  576.1 0.0 copy-done.8
  576.1 0.0 copy-done.9
  576.1 0.6 copy.53
  576.7 0.6 copy.54
  577.3 0.6 copy.55
  578.0 2.7 copy.105
  580.6 0.0 copy-done
  580.6 0.0 copy-start.4
  580.6 0.0 copy-start.5
  580.6 1.7 copy.106
  582.3 0.9 copy-done.4
  583.2 0.0 copy-start.3
  583.2 1.2 copy.107
  584.4 0.0 copy-done.5
  584.4 0.9 copy.108
  585.3 0.7 copy-done.3
  586.1 0.0 copy-start.2
  586.1 1.6 copy.109
  587.7 1.3 copy-done.2
  589.0 1.6 copy.110
  (32 shorter events, 0.4 us)
Async XLA Ops:
  2.2 1.3 copy-start.7
  2.2 2.9 copy-start.1
  2.7 0.8 copy-start.11
  3.5 2.9 copy-start.6
  125.3 0.7 copy-start.10
  400.2 63.2 %copy-start.13 = (s32[24]{0:T(128)S(1)}, s32[24]{0:T(128)}, u32[]{:S(2)}) copy-start(s32[24]{0:T(128)} %param.17) | copy-start | bytes 292
  400.3 63.4 %copy-start.12 = (f32[24]{0:T(128)S(1)}, f32[24]{0:T(128)}, u32[]{:S(2)}) copy-start(f32[24]{0:T(128)} %constant.45) | copy-start | bytes 292
  464.9 111.2 %copy-start.8 = (f32[2,12,24]{2,0,1:T(2,128)S(1)}, f32[2,12,24]{2,0,1:T(2,128)}, u32[]{:S(2)}) copy-start(f32[2,12,24]{2,0,1:T(2,128)} %param.23) | copy-start | bytes 6916
  464.9 111.2 %copy-start.9 = (f32[2,12,24]{2,0,1:T(2,128)S(1)}, f32[2,12,24]{2,0,1:T(2,128)}, u32[]{:S(2)}) copy-start(f32[2,12,24]{2,0,1:T(2,128)} %param.22) | copy-start | bytes 6916
  575.1 5.5 copy-start
  580.6 2.6 copy-start.4
  580.6 3.8 copy-start.5
  583.2 2.8 copy-start.3
  586.1 2.9 copy-start.2
where the time goes:
time: 598 us; the launch traced here: 591 us
  Pallas kernels  561 us (94%)
  local copies, waits for them, and re-layouts  21.5 us (4%)
  other arithmetic  7.38 us (1%)
    pallas_call x2, Pallas kernels, forward_layer(): pl.pallas_call(functools.partial(forward_kernel, plan), grid=(rows + inne...  200 us
    pallas_call x2, Pallas kernels, attend_back(): pl.pallas_call(functools.partial(attend_back_kernel, plan), grid=(rows,),...  127 us
    pallas_call x2, Pallas kernels, wide_back(): pl.pallas_call(functools.partial(wide_back_kernel, plan, inner), grid=(in...  124 us
    pallas_call x1, Pallas kernels, optimizer(): pl.pallas_call(functools.partial(optimizer_kernel, plan), out_shape=(shap...  110 us
    unnamed x59, local copies, waits for them, and re-layouts  16.2 us

commit v1 on v0

--- a/solution.py
+++ b/solution.py
@@ -167,7 +167,7 @@
     return opens, cores, seconds, thirds, [tick + 2 for tick in thirds]
 
 
-ANNOUNCE, FORWARD, FIRST, SECOND, CLOSE = -4, -2, 2, 4, 6
+ANNOUNCE, FORWARD, FIRST, SECOND, CLOSE = -2, -1, 1, 2, 3
 
 
 def sum_scratch(count, part, width, z_count, kind=low):
@@ -376,10 +376,10 @@
             self.start(hop)
 
 
-def gather_scratch(count, rows, width, z_count, kind=low):
+def gather_scratch(count, group, rows, width, z_count, kind=low):
     piece = (2 * rows // z_count, width // 2) if kind == low else (rows // z_count, width)
     return [
-        pltpu.VMEM((count, z_count) + piece, kind),
+        pltpu.VMEM((count, z_count, group) + piece, kind),
         pltpu.SemaphoreType.DMA((count, 2, z_count)),
         pltpu.SemaphoreType.DMA((count, 2)),
         pltpu.SemaphoreType.DMA((count, 2, 2)),
@@ -395,7 +395,10 @@
     def __init__(self, place, source, whole, base, refs):
         self.place, self.source, self.whole, self.base = place, source, whole, base
         self.zr, self.z_sem, self.a_sem, self.b_sem, self.c_sem, self.far_sem = refs
-        self.count, self.z_count = self.zr.shape[0], self.zr.shape[1]
+        self.count, self.z_count, self.group = self.zr.shape[:3]
+
+    def blocks(self, i):
+        return pl.ds(self.base + self.group * i, self.group)
 
     def z_copy(self, i, d):
         place = self.place
@@ -405,7 +408,7 @@
         )
 
     def chunk(self, i, spot):
-        return self.whole.at[self.base + i, spot, self.place.core]
+        return self.whole.at[self.blocks(i), spot, self.place.core]
 
     def first_copy(self, i):
         chunk = self.chunk(i, self.place.spot)
@@ -416,7 +419,7 @@
         return remote(chunk, chunk, self.b_sem.at[i, 0, k], self.b_sem.at[i, 1, k], self.place.near_b)
 
     def core_copy(self, i):
-        chunks = self.whole.at[self.base + i, :, self.place.core]
+        chunks = self.whole.at[self.blocks(i), :, self.place.core]
         return remote(chunks, chunks, self.c_sem.at[i, 0], self.c_sem.at[i, 1], self.place.sibling)
 
     def far_copy(self, i):
@@ -463,11 +466,12 @@
             self.z_copy(i, 2).wait_recv()
             self.far_copy(i).wait_recv()
 
-        pieces = [self.zr[i, k].astype(full) for k in range(self.z_count)]
-        if self.zr.dtype == low:
-            pieces = [unfold(piece) for piece in pieces]
-        whole = jnp.concatenate(pieces, axis=0).astype(self.whole.dtype)
-        self.whole[self.base + i, self.place.spot, self.place.core] = whole
+        for n in range(self.group):
+            pieces = [self.zr[i, k, n].astype(full) for k in range(self.z_count)]
+            if self.zr.dtype == low:
+                pieces = [unfold(piece) for piece in pieces]
+            whole = jnp.concatenate(pieces, axis=0).astype(self.whole.dtype)
+            self.whole[self.base + self.group * i + n, place.spot, place.core] = whole
         self.first_copy(i).start()
         self.second_copy(i, 0).start()
 
@@ -633,7 +637,8 @@
     lines = line_gathers(place, plan.lines, sources[plan.line_at :], targets[plan.line_target_at :], line_refs, plan.z_count)
 
     def keep(i):
-        return pltpu.make_async_copy(w.at[local + i], w_out.at[i], out_sem.at[i])
+        group = gather.group
+        return pltpu.make_async_copy(w.at[gather.blocks(i)], w_out.at[pl.ds(group * i, group)], out_sem.at[i])
 
     def load(j):
         return pltpu.make_async_copy(w_hbm.at[plan.order[j]], w.at[j], w_sem.at[j])
@@ -699,7 +704,7 @@
                 ctxt_ref[here, :] = context.astype(low)
                 lse_ref[0, pl.ds(2 * p + h, 1), :] = largest + jnp.log(total)
             if gather is not None:
-                spots = [n for n in range(pairs) if (n + 1) * row_ticks // pairs > n * row_ticks // pairs]
+                spots = [n * pairs // row_ticks for n in range(row_ticks)]
                 now, which = looked_up(spots, p)
 
                 @pl.when(now)
@@ -755,10 +760,10 @@
                 u_ref[here, :] = active
                 gp_ref[here, :] = slope.astype(low)
                 acc[here, :] += dot_nn(active, matrix(5 + 2 * c))
-            tick(first + i)
             return carry
 
         lax.fori_loop(0, 2, token_step, 0)
+        tick(first)
 
         @pl.when(c == inner - 1)
         def _():
@@ -777,7 +782,7 @@
             lax.fori_loop(0, 4, last, 0)
             if gather is not None:
                 last_tick = gather.count - 1 + CLOSE
-                lax.fori_loop(firsts[-1] + 2, last_tick + 1, lambda t, carry: (tick(t), carry)[1], 0)
+                lax.fori_loop(firsts[-1] + 1, last_tick + 1, lambda t, carry: (tick(t), carry)[1], 0)
                 for line in lines:
                     line.advance(plan.z_count)
                 for i in range(gather.count):
@@ -791,7 +796,7 @@
         self.order = [0, 1, 2, 3]
         for c in range(inner):
             self.order += [4 + c, 4 + inner + c]
-        self.gathered = 0 if shards is None else shards.shape[0]
+        self.gathered, self.group = (0, 1) if shards is None else (shards.shape[0] * shards.shape[1], shards.shape[1])
         self.vectors = vec_shard is not None
         self.lines = [(first, count) for _, first, count in lines]
         self.line_at = int(self.gathered > 0) + int(self.vectors)
@@ -799,20 +804,20 @@
         self.arguments, self.argument_specs, self.results, self.result_specs, self.scratch = [], [], [], [], []
         shape = jax.ShapeDtypeStruct
         if self.gathered:
-            width = 2 * shards.shape[2]
+            width = 2 * shards.shape[3]
             self.arguments.append(shards)
             self.argument_specs.append(IN_VMEM)
             self.results.append(shape((self.gathered, 4, 2, width // 8, width), low))
             self.result_specs.append(ANYWHERE)
-            self.scratch += gather_scratch(self.gathered, width // 8, width, z_count)
+            self.scratch += gather_scratch(shards.shape[0], self.group, width // 8, width, z_count)
         if self.vectors:
-            rows, lanes = vec_shard.shape[1:]
+            rows, lanes = vec_shard.shape[2:]
             self.arguments.append(vec_shard)
             self.argument_specs.append(IN_VMEM)
             for _ in range(2):
                 self.results.append(shape((16, width), full))
                 self.result_specs.append(pl.BlockSpec((16, width), lambda s: (0, 0)))
-            self.scratch += gather_scratch(1, width // 8, lanes, z_count, full)
+            self.scratch += gather_scratch(1, 1, width // 8, lanes, z_count, full)
         for basis, _, count in lines:
             self.arguments.append(basis)
             self.argument_specs.append(ANYWHERE)
@@ -820,7 +825,7 @@
             self.result_specs.append(ANYWHERE)
         self.scratch += line_scratch(len(lines), z_count)
         if self.gathered:
-            self.scratch.append(pltpu.SemaphoreType.DMA((self.gathered,)))
+            self.scratch.append(pltpu.SemaphoreType.DMA((self.gathered // self.group,)))
         if self.vectors:
             self.scratch.append(pltpu.VMEM((1, 4, 2, width // 8, lanes), full))
 
@@ -829,9 +834,9 @@
         now = self.lead + row_ticks
         for c in range(self.inner):
             starts.append(now)
-            needed = 5 + 2 * c - self.local
+            needed = (5 + 2 * c - self.local) // self.group
             firsts.append(max(now, needed + CLOSE + 1) if self.gathered else now)
-            now = firsts[-1] + 2
+            now = firsts[-1] + 1
         return starts, firsts
 
     def split(self, refs):
@@ -1623,68 +1628,78 @@
     folded = folded.reshape(count, 2 * shard_rows, width // 2)
 
     def pick(numbers):
-        return jnp.stack([folded[j] for j in numbers])
+        return jnp.stack([folded[j] for j in numbers]).reshape(len(numbers) // 2, 2, *folded.shape[1:])
 
     head = pick(order + [per_layer + j for j in order[:4]])
     rest = pick([per_layer + j for j in order[4:]])
     vec_shard = vectors.astype(low).astype(full).reshape(layers * vector_rows, shard_rows).T
-    vec_shard = jnp.pad(vec_shard, ((0, 0), (0, lanes - layers * vector_rows)))[None]
+    vec_shard = jnp.pad(vec_shard, ((0, 0), (0, lanes - layers * vector_rows)))[None, None]
     left_low = left_basis.reshape(slots, -1, width).astype(low)
     right_low = right_basis.transpose(0, 2, 1).astype(low)
 
     plan = ForwardPlan(
-        inner, 0, head, vec_shard, vector_rows, [(right_low, 0, 2)], lead=9, row_ticks=3, z_count=z_count
+        inner, 0, head, vec_shard, vector_rows, [(right_low, 0, 2)], lead=5, row_ticks=1, z_count=z_count
     )
     empty_vec = jnp.zeros((16, width), full)
     results = forward_layer(tokens, seg_column, seg_row, empty_vec, jnp.zeros((1, width, width), low), full, plan, 6)
     kept_a = results[:12]
     hidden, weights_a, vec_a, vec_b, right_01 = results[12:]
     weights_a = weights_a.reshape(-1, width, width)
-    plan = ForwardPlan(inner, 4, rest, lines=[(right_low, 2, 2)], lead=0, row_ticks=4, z_count=z_count)
+    plan = ForwardPlan(inner, 4, rest, lines=[(right_low, 2, 1)], lead=0, row_ticks=2, z_count=z_count)
     plan.order = [per_layer + j for j in range(4)]
     results = forward_layer(hidden, seg_column, seg_row, vec_b, weights_a, low, plan, 7)
     kept_b = results[:12]
-    layer_out, weights_b, right_23 = results[12:]
+    layer_out, weights_b, right_2 = results[12:]
     weights_b = weights_b.reshape(-1, width, width)
 
     def cut(grads):
         return grads.reshape(-1, owners // 2, 2, part, width)
 
     size = (part, width)
-    own = 3
-    skip = own % 2
-    pending = 2 * inner - own
-
-    plan = Plan(None, [(right_low, 4, 1), (left_low, 3, 1)], z_count, own, size, wide_ready(own))
-    dw_wide, dr1, da, dvec_wide_b, wide_sum_b, right_4, left_3 = wide_back(
+    own_b, own_a = 4, 3
+
+    def left_over(own):
+        return 2 * inner - own, own % 2
+
+    plan = Plan(None, [(right_low, 3, 1)], z_count, own_b, size, wide_ready(own_b))
+    dw_wide, dr1, da, dvec_wide_b, wide_sum_b, right_3 = wide_back(
         cotangent, kept_b[5:], vec_b, weights_b, (0, 1, 2), plan, 1
     )
-    ready = list(range(pending + 1))
-    plan = Plan(cut(dw_wide), [(left_low, 4, 1)], z_count, 1, size, ready, skip)
-    dw_attend, upstream, dvec_attend_b, attend_sum_b, left_4 = attend_back(
+    pending, skip = left_over(own_b)
+    plan = Plan(cut(dw_wide), [(right_low, 4, 1), (left_low, 3, 1)], z_count, 1, size, list(range(pending + 1)), skip)
+    dw_attend, upstream, dvec_attend_b, attend_sum_b, right_4, left_3 = attend_back(
         da, dr1, hidden, kept_b[:5], seg_column, seg_row, weights_a, per_layer, plan, 2
     )
-    plan = Plan(cut(dw_attend), [(left_low, 0, 1)], z_count, own, size, [0, 1, 2] + wide_ready(own))
-    dw_wide, dr1, da, dvec_wide_a, wide_sum_a, left_0 = wide_back(
+    plan = Plan(
+        cut(dw_attend), [(left_low, 4, 1), (left_low, 0, 1)], z_count, own_a, size, [0, 1, 2] + wide_ready(own_a)
+    )
+    dw_wide, dr1, da, dvec_wide_a, wide_sum_a, left_4, left_0 = wide_back(
         upstream, kept_a[5:], vec_a, weights_a, (4, 5, 2), plan, 3
     )
-    plan = Plan(cut(dw_wide), [(left_low, 1, 1)], z_count, 1, size, ready, skip)
+    pending, skip = left_over(own_a)
+    plan = Plan(cut(dw_wide), [(left_low, 1, 1)], z_count, 1, size, list(range(pending + 1)), skip)
     dw_attend, upstream, dvec_attend_a, attend_sum_a, left_1 = attend_back(
         da, dr1, tokens, kept_a[:5], seg_column, seg_row, weights_a, 0, plan, 5
     )
 
     three = list(range(3))
-    early = [4 + n // 2 + inner * (n % 2) for n in range(own)]
-    late = [4 + c + inner * k for k in range(2) for c in range(inner) if 2 * c + k >= own] + [3]
-    held_order = three + late + [per_layer + j for j in three] + early + [per_layer + j for j in late + early]
+
+    def early(own):
+        return [4 + n // 2 + inner * (n % 2) for n in range(own)]
+
+    def late(own):
+        return [4 + c + inner * k for k in range(2) for c in range(inner) if 2 * c + k >= own] + [3]
+
+    held_order = three + late(own_a) + [per_layer + j for j in three] + early(own_a)
+    held_order += [per_layer + j for j in late(own_b) + early(own_b)]
     rank = jnp.asarray([held_order.index(j) for j in range(count)], jnp.int32)
     table = slot_table(owner, slots, owners).reshape(slots * owners, count)
     held = jnp.sum(table, axis=1)
     index = jnp.where(held > 0, jnp.sum(table * rank, axis=1), count).astype(jnp.int32)
     places = jnp.sum(table * jnp.arange(slots * owners, dtype=jnp.int32)[:, None], axis=0).astype(jnp.int32)
-    bases = (right_01, right_23, right_4, left_0, left_1, left_3, left_4)
-    right_map = [(0, 0), (0, 1), (1, 0), (1, 1), (2, 0)]
-    left_map = [(3, 0), (4, 0), (7, 0), (5, 0), (6, 0)]
+    bases = (right_01, right_2, right_3, right_4, left_0, left_1, left_3, left_4)
+    right_map = [(0, 0), (0, 1), (1, 0), (2, 0), (3, 0)]
+    left_map = [(4, 0), (5, 0), (8, 0), (6, 0), (7, 0)]
     free = list(range(3, slots))
     new_blocks, new_low, first_new, second_new, vec_sum, _ = optimizer(
         index, places, cut(dw_attend), (attend_sum_a, wide_sum_a, attend_sum_b, wide_sum_b),

time: 598 us -> 592 us (0.990)
  Pallas kernels: 561 us -> 555 us
    unnamed x59 -> x61, local copies, waits for them, and re-layouts: 16.2 us -> 16.3 us
where the time goes in v1:
time: 592 us; the launch traced here: 584 us
  Pallas kernels  555 us (94%)
  local copies, waits for them, and re-layouts  22.4 us (4%)
    pallas_call x2, Pallas kernels, forward_layer(): pl.pallas_call(functools.partial(forward_kernel, plan), grid=(rows + inne...  198 us
    pallas_call x2, Pallas kernels, attend_back(): pl.pallas_call(functools.partial(attend_back_kernel, plan), grid=(rows,),...  124 us
    pallas_call x2, Pallas kernels, wide_back(): pl.pallas_call(functools.partial(wide_back_kernel, plan, inner), grid=(in...  122 us
    pallas_call x1, Pallas kernels, optimizer(): pl.pallas_call(functools.partial(optimizer_kernel, plan), out_shape=(shap...  110 us
    unnamed x61, local copies, waits for them, and re-layouts  16.3 us

profile of v1, /device:TPU:0, one launch (start us, length us, event | category | flops | bytes accessed | tf_op | source)
XLA Modules:
  0.0 583.9 jit_solution(7688272240095801526)
XLA Ops:
  0.6 1.6 convert_element_type.40
  2.2 0.2 reshape.147
  2.4 0.1 fusion.8
  2.6 0.0 copy-start.1
  2.7 0.5 fusion.7
  3.6 0.0 copy-start.12
  3.6 0.9 copy-done.1
  4.5 0.0 copy-start.8
  4.5 0.0 copy-start.7
  4.5 1.3 convert_bitcast_fusion.refs_7_.refs_6_.refs_11_.refs_12_
  5.7 0.0 copy-done.12
  5.7 0.0 copy-done.8
  5.7 1.0 copy.105.refs_1_.refs_8_
  6.7 0.6 broadcast_in_dim.47.refs_2_.refs_9_
  7.3 0.0 copy-done.7
  7.4 0.1 copy.125
  7.5 0.1 reshape.159
  7.5 0.6 bitcast_convert_fusion.refs_6_
  8.2 1.1 reshape.146.refs_4_
  9.3 0.6 broadcast_in_dim.48.refs_3_
  9.9 119.0 %layer_forward.2 = (bf16[1024,768]{1,0:T(8,128)(2,1)}, bf16[1024,768]{1,0:T(8,128)(2,1)}, bf16[1024,768]{1,0:T(8,128)(2,1)}, bf16[768,1024]{1,0:T(8,128)(2,1)}, ...) custom-call(bf16[1024,768]{1,0:T(8,128)(2,1)} %refs_2_.1, ...), custom_call_target="tpu_custom_call" | custom-call | flops 16106127360 | bytes 41943040 | tf_op jit(solution)/shard_map/layer_forward/pallas_call | solution.py:895
  129.1 0.0 copy-start.11
  129.1 0.7 copy-done.11
  129.8 79.4 %layer_forward.3 = (bf16[1024,768]{1,0:T(8,128)(2,1)}, bf16[1024,768]{1,0:T(8,128)(2,1)}, bf16[1024,768]{1,0:T(8,128)(2,1)}, bf16[768,1024]{1,0:T(8,128)(2,1)}, ...) custom-call(f32[1024,768]{1,0:T(8,128)} %get-tuple-element.70.refs_0, ...), custom_call_target="tpu_custom_call" | custom-call | flops 16106127360 | bytes 41943040 | tf_op jit(solution)/shard_map/layer_forward/pallas_call | solution.py:895
  209.2 0.0 copy-start.2
  209.2 57.3 %wide_backward.2 = (bf16[2,2,768,768]{3,2,1,0:T(8,128)(2,1)}, f32[1024,768]{1,0:T(8,128)}, bf16[1024,768]{1,0:T(8,128)(2,1)}, f32[16,768]{1,0:T(8,128)}, bf16[4,...) custom-call(bf16[1024,768]{1,0:T(8,128)(2,1)} %refs_0_.3, f32[1024,768]{1,0:T(8,128)} %get-tuple-element.74.refs_1_, ...), custom_call_target="tpu_custom_call" | custom-call | flops 19327352832 | bytes 52428800 | tf_op jit(solution)/shard_map/wide_backward/pallas_call | solution.py:1086
  266.5 0.0 copy-done.2
  266.5 1.3 convert_element_type.44
  267.7 61.2 %attend_backward.2 = (bf16[3,768,768]{2,1,0:T(8,128)(2,1)}, f32[1024,768]{1,0:T(8,128)}, f32[8,768]{1,0:T(8,128)}, bf16[5,48,384]{2,1,0:T(8,128)(2,1)}, bf16[4,1...) custom-call(bf16[1024,768]{1,0:T(8,128)(2,1)} %get-tuple-element.82.refs_0_, ...), custom_call_target="tpu_custom_call" | custom-call | flops 13690208256 | bytes 31457280 | tf_op jit(solution)/shard_map/attend_backward/pallas_call | solution.py:1263
  329.0 64.8 %wide_backward.3 = (bf16[2,3,768,768]{3,2,1,0:T(8,128)(2,1)}, f32[1024,768]{1,0:T(8,128)}, bf16[1024,768]{1,0:T(8,128)(2,1)}, f32[16,768]{1,0:T(8,128)}, bf16[6,...) custom-call(f32[1024,768]{1,0:T(8,128)} %get-tuple-element.90.refs_0_, ...), custom_call_target="tpu_custom_call" | custom-call | flops 19327352832 | bytes 52428800 | tf_op jit(solution)/shard_map/wide_backward/pallas_call | solution.py:1086
  393.8 0.0 copy-start.14
  393.8 0.0 copy-start.13
  393.8 63.2 %attend_backward.3 = (bf16[3,768,768]{2,1,0:T(8,128)(2,1)}, f32[1024,768]{1,0:T(8,128)}, f32[8,768]{1,0:T(8,128)}, bf16[6,48,384]{2,1,0:T(8,128)(2,1)}, bf16[4,1,192,768]{3,2,1,0:T(8,128)(2,1)}) custom-call(bf16[1024,768]{1,0:T(8,128)(2,1)} %get-tuple-element.100.refs_0_, f32[1024,768]{1,0:T(8,128)} %get-tuple-element.101.refs_1_, ...), custom_call_target="tpu_custom_call" | custom-call | flops 13690208256 | bytes 31457280 | tf_op jit(solution)/shard_map/attend_backward/pallas_call | solution.py:1263
  457.0 0.0 copy-done.14
  457.0 0.2 select_reduce_fusion.1
  457.2 0.0 copy-done.13
  457.2 0.1 fusion.1
  457.3 0.6 convert_element_type.48.refs_0_
  457.9 0.5 convert_element_type.50.refs_1_
  458.4 0.0 copy-start.9
  458.4 0.0 copy-start.10
  458.4 109.9 %optimizer.1 = (f32[24,24,768]{2,1,0:T(8,128)}, bf16[24,24,768]{2,1,0:T(8,128)(2,1)}, f32[5,192,768]{2,1,0:T(8,128)}, f32[5,192,768]{2,1,0:T(8,128)}, f32[24,128...) custom-call(s32[40]{0:T(128)} %convert_element_type.48.refs_0_, s32[24]{0:T(128)} %convert_element_type.50.refs_1_, ...), custom_call_target="tpu_custom_call" | custom-call | flops 4529848320 | bytes 41943040 | tf_op jit(solution)/shard_map/optimizer/pallas_call | solution.py:1538
  568.3 0.0 copy-start
  568.3 0.9 slice_bitcast_fusion
  569.2 0.1 copy.118
  569.3 0.0 copy-done.9
  569.3 0.0 copy-done.10
  569.3 0.6 copy.122
  569.9 0.6 copy.123
  570.5 0.6 copy.124
  571.1 2.7 copy.171
  573.8 0.0 copy-done
  573.8 0.0 copy-start.5
  573.8 0.0 copy-start.6
  573.8 1.7 copy.172
  575.5 0.9 copy-done.5
  576.4 0.0 copy-start.4
  576.4 1.2 copy.173
  577.6 0.0 copy-done.6
  577.6 0.9 copy.174
  578.5 0.7 copy-done.4
  579.3 1.6 copy.175
  580.9 1.3 copy-done.3
  582.2 1.6 copy.176
  (56 shorter events, 0.5 us)
Async XLA Ops:
  2.6 1.8 copy-start.1
  3.6 2.1 copy-start.12
  4.5 1.3 copy-start.8
  4.5 2.9 copy-start.7
  129.1 0.7 copy-start.11
  209.2 57.3 %copy-start.2 = (f32[5,8,24,768]{3,2,1,0:T(8,128)S(1)}, f32[5,8,24,768]{3,2,1,0:T(8,128)}, u32[]{:S(2)}) copy-start(f32[5,8,24,768]{3,2,1,0:T(8,128)} %param.18) | copy-start | bytes 8847364
  393.8 63.2 %copy-start.14 = (s32[24]{0:T(128)S(1)}, s32[24]{0:T(128)}, u32[]{:S(2)}) copy-start(s32[24]{0:T(128)} %param.17) | copy-start | bytes 292
  393.8 63.4 %copy-start.13 = (f32[24]{0:T(128)S(1)}, f32[24]{0:T(128)}, u32[]{:S(2)}) copy-start(f32[24]{0:T(128)} %constant.45) | copy-start | bytes 292
  458.4 110.9 %copy-start.9 = (f32[2,12,24]{2,0,1:T(2,128)S(1)}, f32[2,12,24]{2,0,1:T(2,128)}, u32[]{:S(2)}) copy-start(f32[2,12,24]{2,0,1:T(2,128)} %param.23) | copy-start | bytes 6916
  458.4 110.9 %copy-start.10 = (f32[2,12,24]{2,0,1:T(2,128)S(1)}, f32[2,12,24]{2,0,1:T(2,128)}, u32[]{:S(2)}) copy-start(f32[2,12,24]{2,0,1:T(2,128)} %param.22) | copy-start | bytes 6916
  568.3 5.5 copy-start
  573.8 2.6 copy-start.5
  573.8 3.8 copy-start.6
  576.4 2.8 copy-start.4
  579.3 2.9 copy-start.3
